TPU v7x, 32 devices: a whole 2x2x4 slice. The times are simulated.
32 devices in a mesh: seq: 4 (over y, core), exp: 4 (over z), rep: 2 (over x).
Axes of the slice: x: 2, y: 2, z: 4, core: 2. Of those that a mesh axis runs over, the one named last changes fastest.
Arguments:
- queries: bfloat16 [512, 6144], P('seq'), may hold values from -80 to 80
- keys: bfloat16 [512, 1024], P('seq'), may hold values from -4.2 to 4.2
- values: bfloat16 [512, 1024], P('seq'), may hold values from -6.2 to 6.2
- lengths: int32 [4], replicated, may hold values from 1 to 256, 512 in all
- expert_ids: int32 [512, 4], P('seq'), may hold values from 0 to 15, all different within a row; in each aligned block of 128 rows (0 to 127, 128 to 255, ...) at most 34 rows name the same one
- gate_share: float32 [512, 4], P('seq'), may hold values from 0.2 to 1
- gate_up: bfloat16 [16, 6144, 2, 5376], P('exp', 'rep', None, 'seq'), may hold values from -0.15625 to 0.15625
- down_t: bfloat16 [16, 6144, 5376], P('exp', 'rep', 'seq'), may hold values from -0.15625 to 0.15625
Outputs:
- moe_out: bfloat16 [512, 6144], P(('seq', 'exp'), 'rep')
Inputs may be any that keep to these rules, and one draw needn't show every extreme that they name: The lengths sum to 512; each is at most 256, and one is exactly 256. `expert_ids`: each token names 4 different experts. Among the 128 tokens of one device (aligned blocks of 128 positions), no expert is named more than 34 times, a bound that some block reaches.
All inputs are finite; a program needn't handle non-finite values.
Results may differ from a plain program's by a relative error of at most 0.035.
Values may be sent and summed in bfloat16 or wider, within the bound.
A program may use at most 192 MiB of HBM per device.

v0:
```python
import jax
import jax.numpy as jnp
from jax import lax
from jax.sharding import PartitionSpec as P

HEADS = 48
KV = 8
HD = 128
TOPK = 4
REACH = 2
CAP = 34


def segment_ids(lens, length):
    ends = jnp.cumsum(lens)
    places = jnp.arange(length, dtype=jnp.int32)
    return jnp.sum((places[:, None] >= ends[None, :]).astype(jnp.int32), axis=1)


def softmax_rows(scores):
    top = jnp.max(scores, axis=-1, keepdims=True)
    weights = jnp.exp(scores - top)
    return (weights / jnp.sum(weights, axis=-1, keepdims=True)).astype(jnp.bfloat16)


def earlier(blocks_arr, back, fill):
    padding = jnp.full((back,) + blocks_arr.shape[1:], fill, blocks_arr.dtype)
    return jnp.concatenate([padding, blocks_arr[: blocks_arr.shape[0] - back]], 0)


def widen(blocks_arr, fill):
    parts = [earlier(blocks_arr, back, fill) for back in range(REACH, 0, -1)]
    return jnp.concatenate(parts + [blocks_arr], 1)


def per_device(queries, keys, values, lengths, expert_ids, gate_share, gate_up, down_t):
    n_seq = lax.axis_size("seq")
    tok = queries.shape[0]
    length = tok * n_seq
    owned = gate_up.shape[0]
    cols = gate_up.shape[1]
    rep_index = lax.axis_index("rep")
    segment = segment_ids(lengths, length)
    local_heads = HEADS // n_seq
    repeat = max(1, n_seq // KV)
    slots = KV * repeat // n_seq
    per_slot = local_heads // slots
    q_send = queries.reshape(tok, n_seq, local_heads * HD)
    kv_rows = jnp.concatenate([keys.reshape(tok, KV, HD), values.reshape(tok, KV, HD)], axis=2)
    kv_send = jnp.repeat(kv_rows, repeat, axis=1).reshape(tok, n_seq, slots * 2 * HD)
    q_all, kv_all = (
        lax.all_to_all(q_send, "seq", split_axis=1, concat_axis=0, tiled=True),
        lax.all_to_all(kv_send, "seq", split_axis=1, concat_axis=0, tiled=True),
    )
    q_tile = q_all.reshape(n_seq, tok, slots, per_slot, HD)
    kv_wide = widen(kv_all.reshape(n_seq, tok, slots, 2 * HD), 0)
    seg_tile = segment.reshape(n_seq, tok)
    seg_keys = widen(seg_tile, -1)
    q_pos = jnp.arange(length, dtype=jnp.int32).reshape(n_seq, tok)
    k_pos = q_pos[:, :1] - REACH * tok + jnp.arange((REACH + 1) * tok, dtype=jnp.int32)[None, :]
    allowed = (seg_tile[:, :, None] == seg_keys[:, None, :]) & (
        k_pos[:, None, :] <= q_pos[:, :, None]
    )

    def one_head(q_head):
        scores = jnp.einsum(
            "ntsd,nksd->nstk", q_head, kv_wide[..., :HD], preferred_element_type=jnp.float32
        ) * HD ** (-0.5)
        scores = jnp.where(allowed[:, None], scores, -jnp.inf)
        probs = softmax_rows(scores)
        mixed_rows = jnp.einsum(
            "nstk,nksd->ntsd", probs, kv_wide[..., HD:], preferred_element_type=jnp.float32
        )
        return mixed_rows.astype(jnp.bfloat16)

    result = lax.map(one_head, jnp.moveaxis(q_tile, 3, 0))
    result = jnp.moveaxis(result, 0, 3).reshape(length, local_heads * HD)
    attended = lax.all_to_all(result, "seq", split_axis=0, concat_axis=1, tiled=True)
    local_cols = lax.dynamic_slice_in_dim(attended, rep_index * cols, cols, 1)
    routes = tok * TOPK
    mine = lax.axis_index("exp") * owned + jnp.arange(owned, dtype=jnp.int32)
    ids = expert_ids.reshape(routes)
    shares = gate_share.reshape(routes)
    match = (ids[None, :] == mine[:, None]).astype(jnp.int32)
    rank = jnp.cumsum(match, axis=1) - match
    slot_hit = match[:, None, :] * (
        rank[:, None, :] == jnp.arange(CAP, dtype=jnp.int32)[None, :, None]
    ).astype(jnp.int32)
    token_of = jnp.arange(routes, dtype=jnp.int32) // TOPK
    token_for = jnp.sum(slot_hit * token_of[None, None, :], axis=2)
    live = jnp.sum(slot_hit, axis=2)
    share_for = jnp.sum(slot_hit.astype(jnp.float32) * shares[None, None, :], axis=2)
    picked = local_cols[token_for] * live[..., None].astype(jnp.bfloat16)
    both_part = jnp.einsum(
        "ecd,edgf->ecgf",
        lax.all_gather(picked, "seq", axis=1, tiled=True),
        gate_up,
        preferred_element_type=jnp.float32,
    )
    both_part = lax.optimization_barrier(both_part.astype(jnp.bfloat16)).astype(jnp.float32)
    both = lax.psum(both_part.astype(jnp.bfloat16), "rep").astype(jnp.float32)
    hidden = (jax.nn.silu(both[:, :, 0]) * both[:, :, 1]).astype(jnp.bfloat16)
    down_part = jnp.einsum("ecf,edf->ecd", hidden, down_t, preferred_element_type=jnp.float32)
    down_part = lax.optimization_barrier(down_part.astype(jnp.bfloat16)).astype(jnp.float32)
    expert_out = lax.psum_scatter(
        down_part.astype(jnp.bfloat16), "seq", scatter_dimension=1, tiled=True
    ).astype(jnp.float32)
    weighted = expert_out * (live.astype(jnp.float32) * share_for)[..., None]
    term = jax.ops.segment_sum(
        weighted.reshape(owned * CAP, cols), token_for.reshape(owned * CAP), num_segments=tok
    )
    term = lax.optimization_barrier(term.astype(jnp.bfloat16)).astype(jnp.float32)
    mixed = lax.psum_scatter(term.astype(jnp.bfloat16), "exp", scatter_dimension=0, tiled=True)
    return mixed


def solution(mesh):
    in_specs = (
        P("seq", None),
        P("seq", None),
        P("seq", None),
        P(),
        P("seq", None),
        P("seq", None),
        P("exp", "rep", None, "seq"),
        P("exp", "rep", "seq"),
    )
    out_specs = P(("seq", "exp"), "rep")
    return jax.shard_map(
        per_device, mesh=mesh, in_specs=in_specs, out_specs=out_specs, check_vma=False
    )
```

profile of v0, /device:TPU:0, one launch (start us, length us, event | category | flops | bytes accessed | tf_op | source)
XLA Modules:
  0.0 391.7 jit_solution(7818532921028591630)
XLA Ops:
  6.5 1.2 copy.90
  7.8 1.1 copy.91
  8.9 0.8 pad_maximum_fusion
  9.7 4.2 %all-to-all-start.1 = ((bf16[128,4,512]{0,2,1:T(8,128)(2,1)}), bf16[128,4,512]{0,2,1:T(8,128)(2,1)S(1)}, u32[]{:S(2)}, u32[]{:S(2)}) async-start(bf16[128,4,512]{0,2,1:T(8,128)(2,1)} %bitcast.7), calls=%async_computation.1 | async-start | bytes 1048576 | tf_op jit(solution)/shard_map/all_to_all | solution.py:53
  14.2 1.6 copy.74
  15.9 6.9 %all-to-all-done.1 = bf16[128,4,512]{0,2,1:T(8,128)(2,1)S(1)} async-done(((bf16[128,4,512]{0,2,1:T(8,128)(2,1)}), bf16[128,4,512]{0,2,1:T(8,128)(2,1)S(1)}, u32[]{:S(2)}, u32[]{:S(2)}) %all-to-all-start.1) | async-done | bytes 524320 | tf_op jit(solution)/shard_map/all_to_all | solution.py:53
  22.8 4.3 %all-to-all-start = ((bf16[128,4,1536]{0,2,1:T(8,128)(2,1)}), bf16[128,4,1536]{0,2,1:T(8,128)(2,1)}, u32[]{:S(2)}, u32[]{:S(2)}) async-start(bf16[128,4,1536]{0,2,1:T(8,128)(2,1)} %bitcast), calls=%async_computation | async-start | bytes 3145728 | tf_op jit(solution)/shard_map/all_to_all | solution.py:52
  27.5 1.2 reduce-window.18
  29.3 1.6 copy.78
  30.9 16.4 %all-to-all-done = bf16[128,4,1536]{0,2,1:T(8,128)(2,1)} async-done(((bf16[128,4,1536]{0,2,1:T(8,128)(2,1)}), bf16[128,4,1536]{0,2,1:T(8,128)(2,1)}, u32[]{:S(2)}, u32[]{:S(2)}) %all-to-all-start) | async-done | bytes 1572896 | tf_op jit(solution)/shard_map/all_to_all | solution.py:52
  47.3 38.0 %while.11 = (s32[]{:T(128)}, bf16[6,4,128,2,128]{2,4,0,3,1:T(8,128)(2,1)}, bf16[6,4,128,2,128]{2,4,0,3,1:T(8,128)(2,1)}, bf16[4,384,2,256]{3,1,2,0:T(8,128)(2,1)...) while((s32[]{:T(128)}, ...), condition=%wide.region_8.9_spmd.clone, body=%wide.region_5.8_spmd.clone.sunk | while | flops 204407168 | bytes 13000841 | solution.py:76
  47.5 3.3 fusion.60
  50.9 1.8 fusion.61
  52.9 0.8 constant_dynamic-update-slice_fusion.2
  53.9 3.3 fusion.60
  57.2 1.8 fusion.61
  59.2 0.8 constant_dynamic-update-slice_fusion.2
  60.2 3.3 fusion.60
  63.5 1.8 fusion.61
  65.6 0.8 constant_dynamic-update-slice_fusion.2
  66.6 3.3 fusion.60
  69.9 1.8 fusion.61
  71.9 0.8 constant_dynamic-update-slice_fusion.2
  72.9 3.3 fusion.60
  76.2 1.8 fusion.61
  78.3 0.7 constant_dynamic-update-slice_fusion.2
  79.2 3.3 fusion.60
  82.6 1.8 fusion.61
  84.6 0.7 constant_dynamic-update-slice_fusion.2
  85.3 3.6 all-to-all-start.2
  89.5 1.2 select_reduce_fusion
  91.0 18.0 %all-to-all-done.2 = bf16[4,128,1536]{1,2,0:T(8,128)(2,1)S(1)} async-done(((bf16[4,128,1536]{1,2,0:T(8,128)(2,1)}), bf16[4,128,1536]{1,2,0:T(8,128)(2,1)S(1)}, u32[]{:S(2)}, u32[]{:S(2)}) %all-to-all-start.2) | async-done | bytes 1572896 | tf_op jit(solution)/shard_map/all_to_all | solution.py:78
  109.3 1.1 gather_fusion
  110.8 1.6 copy.83
  112.4 30.7 %all-gather.2.cloned.1.call-done = bf16[4,136,3072]{2,0,1:T(4,128)(2,1)} async-done(((bf16[4,34,3072]{2,0,1:T(4,128)(2,1)}), bf16[4,136,3072]{2,0,1:T(4,128)(2,1)}) %all-gather.2.cloned.1.call-update) | async-done | bytes 3342352 | tf_op jit(solution)/shard_map/all_gather | solution.py:96
  143.1 29.2 %convolution_convert_fusion.2 = bf16[4,136,2,1344]{3,1,2,0:T(8,128)(2,1)} fusion(bf16[4,3072,2,1344]{1,3,2,0:T(8,128)(2,1)} %param.16, bf16[4,136,3072,1]{2,0,1,3:T(4,128)(2,1)} %bitcast.76), kind=kOutput, calls=%fused_computation.24 | convolution fusion | flops 8985661440 | bytes 72327168 | tf_op jit(solution)/shard_map/ecd,edgf->ecgf/dot_general | solution.py:94
  172.5 83.9 %all-reduce.8.cloned.1.call-done = bf16[4,136,2,1344]{3,1,2,0:T(8,128)(2,1)} async-done(((bf16[4,136,2,1344]{3,1,2,0:T(8,128)(2,1)}), bf16[4,136,2,1344]{3,1,2,0:T(8,128)(2,1)}) %all-reduce.8.cloned.1.call-update) | async-done | bytes 2924560 | tf_op jit(solution)/shard_map/psum | solution.py:101
  256.5 4.9 %convert_element_type.73 = f32[4,136,2,1344]{3,1,2,0:T(8,128)} convert(bf16[4,136,2,1344]{3,1,2,0:T(8,128)(2,1)} %all-reduce.8.cloned.1.call-done) | non-fusion elementwise | flops 1462272 | bytes 8773632 | tf_op jit(solution)/shard_map/convert_element_type | solution.py:101
  261.3 15.1 %convolution_convert_fusion.1 = bf16[4,136,3072]{2,1,0:T(8,128)(2,1)S(1)} fusion(bf16[4,3072,1344]{1,2,0:T(8,128)(2,1)} %param.17, f32[4,136,2,1344]{3,1,2,0:T(8,128)} %convert_element_type.73), kind=kOutput, calls=%fused_computation.23 | convolution fusion | flops 4498157568 | bytes 42221568 | tf_op jit(solution)/shard_map/ecf,edf->ecd/dot_general | solution.py:103
  276.4 4.3 %copy.86 = bf16[4,136,3072]{2,0,1:T(4,128)(2,1)} copy(bf16[4,136,3072]{2,1,0:T(8,128)(2,1)S(1)} %convolution_convert_fusion.1) | data formatting | bytes 6684672 | tf_op jit(solution)/shard_map/optimization_barrier | solution.py:104
  281.7 0.6 dynamic-slice
  283.1 69.5 %all-reduce.10.cloned.1.call-done = bf16[4,136,3072]{2,0,1:T(4,128)(2,1)} async-done(((bf16[4,136,3072]{2,0,1:T(4,128)(2,1)}), bf16[4,136,3072]{2,0,1:T(4,128)(2,1)}) %all-reduce.10.cloned.1.call-update) | async-done | bytes 3342352
  352.6 1.6 convert_multiply_fusion
  354.2 1.0 copy.88
  355.2 1.4 reshape.254
  356.5 4.0 %scatter_custom_fusion = f32[128,3072]{1,0:T(8,128)S(1)} fusion(s32[136]{0:T(256)S(1)} %reshape.252, f32[136,3072]{1,0:T(8,128)} %reshape.254, f32[]{:T(128)} %constant.59.clone.1), kind=kCustom, calls=%fused_computation.38 | custom fusion | flops 417792 | bytes 1573376 | tf_op jit(solution)/shard_map/scatter-add | solution.py:109
  360.6 1.0 convert_element_type.79
  361.6 23.6 %reduce-scatter.2.cloned.1.call-done = bf16[32,3072]{1,0:T(8,128)(2,1)} async-done(((bf16[128,3072]{1,0:T(8,128)(2,1)}), bf16[32,3072]{1,0:T(8,128)(2,1)}) %reduce-scatter.2.cloned.1.call-update) | async-done | bytes 196624 | tf_op jit(solution)/shard_map/reduce_scatter | solution.py:113
  (80 shorter events, 6.5 us)
Async XLA Ops:
  6.5 7.4 %copy-start.2 = (s32[128,4]{0,1:T(4,128)S(1)}, s32[128,4]{0,1:T(4,128)}, u32[]{:S(2)}) copy-start(s32[128,4]{0,1:T(4,128)} %param.14) | copy-start | bytes 6148
  6.5 7.7 %copy-start = (bf16[128,6144]{1,0:T(8,128)(2,1)S(1)}, bf16[128,6144]{1,0:T(8,128)(2,1)}, u32[]{:S(2)}) copy-start(bf16[128,6144]{1,0:T(8,128)(2,1)} %param.10) | copy-start | bytes 4718596
  9.7 13.1 %all-to-all-start.1 = ((bf16[128,4,512]{0,2,1:T(8,128)(2,1)}), bf16[128,4,512]{0,2,1:T(8,128)(2,1)S(1)}, u32[]{:S(2)}, u32[]{:S(2)}) async-start(bf16[128,4,512]{0,2,1:T(8,128)(2,1)} %bitcast.7), calls=%async_computation.1 | async-start | bytes 1048576 | tf_op jit(solution)/shard_map/all_to_all | solution.py:53
  15.8 11.5 %copy-start.4 = (s32[4]{0:T(128)S(1)}, s32[4]{0:T(128)}, u32[]{:S(2)}) copy-start(s32[4]{0:T(128)} %param.13) | copy-start | bytes 52
  22.8 24.5 %all-to-all-start = ((bf16[128,4,1536]{0,2,1:T(8,128)(2,1)}), bf16[128,4,1536]{0,2,1:T(8,128)(2,1)}, u32[]{:S(2)}, u32[]{:S(2)}) async-start(bf16[128,4,1536]{0,2,1:T(8,128)(2,1)} %bitcast), calls=%async_computation | async-start | bytes 3145728 | tf_op jit(solution)/shard_map/all_to_all | solution.py:52
  47.5 3.3 copy-start.1
  53.9 3.3 copy-start.1
  60.2 3.3 copy-start.1
  66.6 3.3 copy-start.1
  72.9 3.3 copy-start.1
  79.2 3.3 copy-start.1
  85.3 23.6 %all-to-all-start.2 = ((bf16[4,128,1536]{1,2,0:T(8,128)(2,1)}), bf16[4,128,1536]{1,2,0:T(8,128)(2,1)S(1)}, u32[]{:S(2)}, u32[]{:S(2)}) async-start(bf16[4,128,1536]{1,2,0:T(8,128)(2,1)} %bitcast.81), calls=%async_computation.2 | async-start | bytes 3145728 | tf_op jit(solution)/shard_map/all_to_all | solution.py:78
  88.9 54.2 %all-gather.2.cloned.1.call-start = ((), (), s32[]{:S(2)}) async-start(), calls=%async_computation.4 | async-start | bytes 4177920 | tf_op jit(solution)/shard_map/all_gather | solution.py:96
  112.3 144.1 %all-reduce.8.cloned.1.call-start = ((), (), s32[]{:S(2)}) async-start(), calls=%async_computation.5 | async-start | bytes 6127616 | tf_op jit(solution)/shard_map/psum | solution.py:101
  172.3 180.3 %all-reduce.10.cloned.1.call-start = ((), (), s32[]{:S(2)}) async-start(), calls=%async_computation.7 | async-start | bytes 6684672
  280.7 0.7 copy-start.3
  280.7 0.9 copy-start.5
  280.8 104.4 %reduce-scatter.2.cloned.1.call-start = ((), (), s32[]{:S(2)}) async-start(), calls=%async_computation.6 | async-start | bytes 983040 | tf_op jit(solution)/shard_map/reduce_scatter | solution.py:113
Sparse Core Ops, SparseCore 0:
  112.5 30.5 all-gather.1
  172.4 83.9 all-reduce.7
  280.9 71.6 all-reduce.9
  361.7 23.3 reduce-scatter.1
where the time goes:
time: 393 us; the launch traced here: 392 us
  waiting for transfers between devices  249 us (63%)
  matrix products  75.1 us (19%)
  local copies, waits for them, and re-layouts  23.4 us (6%)
  other arithmetic  17.5 us (4%)
  between operations  14 us (4%)
  starting transfers between devices  12.5 us (3%)
    psum x1, waiting for transfers between devices, per_device(): both = lax.psum(both_part.astype(jnp.bfloat16), 'rep').astype(jnp.float32)  83.9 us
    unnamed x5, waiting for transfers between devices  69.6 us
    all_gather x1, waiting for transfers between devices, per_device(): lax.all_gather(picked, 'seq', axis=1, tiled=True)  30.7 us
    dot_general x1, matrix products, per_device(): jnp.einsum('ecd,edgf->ecgf', lax.all_gather(picked, 'seq', axis=1, tiled=...  29.2 us
    reduce_scatter x1, waiting for transfers between devices, per_device(): lax.psum_scatter(term.astype(jnp.bfloat16), 'exp', scatter_dimension=0, t...  23.6 us
    sub x6, matrix products, softmax_rows(): weights = jnp.exp(scores - top)  19.9 us
    all_to_all x1, waiting for transfers between devices, per_device(): lax.all_to_all(result, 'seq', split_axis=0, concat_axis=1, tiled=True)  18 us
    all_to_all x1, waiting for transfers between devices, per_device(): lax.all_to_all(q_send, 'seq', split_axis=1, concat_axis=0, tiled=True)  16.4 us
  transfers between devices with their start and end apart: 7, of which 7 were waited for; matrix products, arithmetic and copies ran while one was open for 2% of the time, Pallas kernels for 0%

commit v1 on v0

v1 whole, which is shorter than its diff:
```python
import jax
import jax.numpy as jnp
from jax import lax
from jax.sharding import PartitionSpec as P

HEADS = 48
KV = 8
HD = 128
TOPK = 4
REACH = 2
CAP = 34
GROUP = HEADS // KV
TAIL_PIECES = 2


def swap(x, axis, distance):
    n = lax.axis_size(axis)
    return lax.ppermute(x, axis, [(i, i ^ distance) for i in range(n)])


def shift(x, axis, distance):
    n = lax.axis_size(axis)
    return lax.ppermute(x, axis, [(i, i + distance) for i in range(n - distance)])


def bits_down(n):
    return [1 << b for b in reversed(range(n.bit_length() - 1))]


def gather_swapped(x, axis):
    n = lax.axis_size(axis)
    x = x[None]
    for bit in bits_down(n):
        other = swap(x, axis, bit)
        size = x.shape[0]
        both = jnp.stack([x, other], 1)
        x = both.reshape((2 * size,) + x.shape[1:]) if size > 1 else both[0]
    return x


def attend(queries, keys, values, lengths, kv_here, split):
    tok = queries.shape[0]
    s = lax.axis_index("seq")
    e = lax.axis_index("exp")
    r = lax.axis_index("rep")
    n_exp = lax.axis_size("exp")
    per = max(1, kv_here // n_exp)
    rows = tok // split
    head = r * kv_here + (e // split) * per
    k = lax.dynamic_slice_in_dim(keys, head * HD, per * HD, 1)
    v = lax.dynamic_slice_in_dim(values, head * HD, per * HD, 1)
    kv = jnp.concatenate([k, v], axis=1)
    wide = [shift(kv, "seq", back) for back in range(REACH, 0, -1)] + [kv]
    wide = jnp.concatenate(wide, 0)
    span = (REACH + 1) * tok
    k_wide = wide[:, : per * HD].reshape(span, per, HD)
    v_wide = wide[:, per * HD :].reshape(span, per, HD)
    q = lax.dynamic_slice(
        queries, ((e % split) * rows, head * GROUP * HD), (rows, per * GROUP * HD)
    ).reshape(rows, per, GROUP, HD)
    ends = jnp.cumsum(lengths)
    q_pos = s * tok + (e % split) * rows + jnp.arange(rows, dtype=jnp.int32)
    k_pos = (s - REACH) * tok + jnp.arange(span, dtype=jnp.int32)
    q_seg = jnp.sum((q_pos[:, None] >= ends[None, :]).astype(jnp.int32), axis=1)
    k_seg = jnp.sum((k_pos[:, None] >= ends[None, :]).astype(jnp.int32), axis=1)
    allowed = (
        (q_seg[:, None] == k_seg[None, :])
        & (k_pos[None, :] <= q_pos[:, None])
        & (k_pos[None, :] >= 0)
    )
    scores = jnp.einsum(
        "tpjd,kpd->pjtk", q, k_wide, preferred_element_type=jnp.float32
    ) * HD ** (-0.5)
    scores = jnp.where(allowed[None, None], scores, -jnp.inf)
    top = jnp.max(scores, axis=-1, keepdims=True)
    weights = jnp.exp(scores - top)
    probs = (weights / jnp.sum(weights, axis=-1, keepdims=True)).astype(jnp.bfloat16)
    out = jnp.einsum("pjtk,kpd->tpjd", probs, v_wide, preferred_element_type=jnp.float32)
    return out.astype(jnp.bfloat16).reshape(rows, per * GROUP * HD)


def gather_tokens(own, tok, cols, split):
    n_seq = lax.axis_size("seq")
    n_exp = lax.axis_size("exp")
    e = lax.axis_index("exp")
    rows, width = own.shape
    pieces = [own] + [swap(own, "exp", d) for d in range(1, n_exp)]
    bunch = max(1, n_exp // 4)
    full = jnp.zeros((n_seq, tok, cols), jnp.bfloat16)
    for first in range(0, n_exp, bunch):
        held = jnp.stack(pieces[first : first + bunch])
        got = gather_swapped(held, "seq")
        for j in range(bunch):
            at = e ^ (first + j)
            full = lax.dynamic_update_slice(
                full, got[:, j], (0, (at % split) * rows, (at // split) * width)
            )
    return full.reshape(n_seq * tok, cols)


def per_device(queries, keys, values, lengths, expert_ids, gate_share, gate_up, down_t):
    n_seq = lax.axis_size("seq")
    n_exp = lax.axis_size("exp")
    n_rep = lax.axis_size("rep")
    tok = queries.shape[0]
    owned, cols = gate_up.shape[0], gate_up.shape[1]
    e = lax.axis_index("exp")
    r = lax.axis_index("rep")
    kv_here = cols // (GROUP * HD)
    split = max(1, n_exp // kv_here)

    table = jnp.concatenate([expert_ids.astype(jnp.float32).T, gate_share.T], 0)
    table = gather_swapped(table, "seq")
    ids = table[:, :TOPK].astype(jnp.int32)
    shares = table[:, TOPK:]
    mine = e * owned + jnp.arange(owned, dtype=jnp.int32)
    hit = ids[None] == mine[:, None, None, None]
    match = jnp.any(hit, axis=2)
    share = jnp.sum(jnp.where(hit, shares[None], 0.0), axis=2)
    count = match.astype(jnp.int32)
    rank = jnp.cumsum(count, axis=2) - count
    block = jnp.arange(n_seq, dtype=jnp.int32)[None, :, None]
    key = jnp.where(match, block * CAP + rank, -1)
    rows = n_seq * CAP
    part = rows // n_rep
    at = jnp.arange(rows, dtype=jnp.int32)
    slot = (r ^ (at // part)) * part + at % part
    pick = (key.reshape(owned, 1, n_seq * tok) == slot[None, :, None]).astype(jnp.bfloat16)

    def turned(x):
        cut = x.reshape(owned, n_seq, n_exp, tok // n_exp)
        order = e ^ jnp.arange(n_exp, dtype=jnp.int32)
        return jnp.take(cut, order, axis=2).reshape(owned, n_seq * tok)

    key_out, share_out = turned(key), turned(share)
    spread = jnp.where(
        key_out.T[:, :, None] == slot[None, None, :], share_out.T[:, :, None], 0.0
    ).astype(jnp.bfloat16).reshape(n_seq * tok, owned * rows)

    own = attend(queries, keys, values, lengths, kv_here, split)
    tokens = gather_tokens(own, tok, cols, split)

    outs = []
    for i in range(owned):
        picked = jnp.dot(pick[i], tokens, preferred_element_type=jnp.float32).astype(jnp.bfloat16)
        both = jnp.einsum("rd,dgf->grf", picked, gate_up[i], preferred_element_type=jnp.float32)
        both = both.astype(jnp.bfloat16)
        total = both[:, :part].astype(jnp.float32)
        for d in range(1, n_rep):
            got = swap(both[:, d * part : (d + 1) * part], "rep", d)
            total = total + got.astype(jnp.float32)
        hidden = (jax.nn.silu(total[0]) * total[1]).astype(jnp.bfloat16)
        hidden = jnp.concatenate([hidden] + [swap(hidden, "rep", d) for d in range(1, n_rep)], 0)
        down = jnp.einsum("rf,df->rd", hidden, down_t[i], preferred_element_type=jnp.float32)
        outs.append(down.astype(jnp.bfloat16))
    outs = jnp.concatenate(outs, 0)

    results = []
    wide = cols // TAIL_PIECES
    for c in range(TAIL_PIECES):
        term = jnp.dot(
            spread, outs[:, c * wide : (c + 1) * wide], preferred_element_type=jnp.float32
        ).astype(jnp.bfloat16).reshape(n_seq, tok, wide)
        for bit in reversed(bits_down(n_seq)):
            pairs = term.reshape(term.shape[0] // 2, 2, tok, wide)
            got = swap(pairs[:, 1], "seq", bit)
            term = (pairs[:, 0].astype(jnp.float32) + got.astype(jnp.float32)).astype(jnp.bfloat16)
        chunks = term.reshape(n_exp, tok // n_exp, wide)
        total = chunks[0].astype(jnp.float32)
        for d in range(1, n_exp):
            total = total + swap(chunks[d], "exp", d).astype(jnp.float32)
        results.append(total.astype(jnp.bfloat16))
    return jnp.concatenate(results, 1)


def solution(mesh):
    in_specs = (
        P("seq", None),
        P("seq", None),
        P("seq", None),
        P(),
        P("seq", None),
        P("seq", None),
        P("exp", "rep", None, "seq"),
        P("exp", "rep", "seq"),
    )
    out_specs = P(("seq", "exp"), "rep")
    return jax.shard_map(
        per_device, mesh=mesh, in_specs=in_specs, out_specs=out_specs, check_vma=False
    )
```

time: 393 us -> 186 us (0.47)
  waiting for transfers between devices: 249 us -> 64.1 us
  starting transfers between devices: 12.5 us -> 34.7 us
  between operations: 14 us -> 0.65 us
  local copies, waits for them, and re-layouts: 23.4 us -> 10.2 us
  matrix products: 75.1 us -> 66.1 us
  other arithmetic: 17.5 us -> 9.79 us
    psum x1 -> x0, waiting for transfers between devices: 83.9 us -> none  [per_device(): both = lax.psum(both_part.astype(jnp.bfloat16), 'rep').astype(jnp.float32)]
    unnamed x5 -> x0, waiting for transfers between devices: 69.6 us -> none
    ppermute x0 -> x33, waiting for transfers between devices: none -> 64.1 us  [the longest x31 64.1 us: swap(): return lax.ppermute(x, axis, [(i, i ^ distance) for i in range(n)])]
    all_to_all x3 -> x0, waiting for transfers between devices: 41.2 us -> none  [the longest x1 18 us: per_device(): lax.all_to_all(result, 'seq', split_axis=0, concat_axis=1, tiled=True)]
    ppermute x0 -> x33, starting transfers between devices: none -> 34.7 us  [the longest x31 27.9 us: swap(): return lax.ppermute(x, axis, [(i, i ^ distance) for i in range(n)])]
    all_gather x1 -> x0, waiting for transfers between devices: 30.7 us -> none  [per_device(): lax.all_gather(picked, 'seq', axis=1, tiled=True)]
    reduce_scatter x1 -> x0, waiting for transfers between devices: 23.6 us -> none  [per_device(): lax.psum_scatter(term.astype(jnp.bfloat16), 'exp', scatter_dimension=0, t...]
    sub x6 -> x0, matrix products: 19.9 us -> none  [softmax_rows(): weights = jnp.exp(scores - top)]
  transfers between devices with their start and end apart: 7 -> 33, of which waited for: 7 -> 18; matrix products, arithmetic and copies ran while one was open for 2% -> 22% of each run, Pallas kernels for 0% -> 0%
where the time goes in v1:
time: 186 us
  matrix products  66.1 us (36%)
  waiting for transfers between devices  64.1 us (34%)
  starting transfers between devices  34.7 us (19%)
  local copies, waits for them, and re-layouts  10.2 us (5%)
  other arithmetic  9.79 us (5%)
    ppermute x31, waiting for transfers between devices, swap(): return lax.ppermute(x, axis, [(i, i ^ distance) for i in range(n)])  64.1 us
    dot_general x4, matrix products, per_device(): jnp.einsum('rd,dgf->grf', picked, gate_up[i], preferred_element_type=jnp....  43.2 us
    ppermute x31, starting transfers between devices, swap(): return lax.ppermute(x, axis, [(i, i ^ distance) for i in range(n)])  27.9 us
    dot_general x4, matrix products, per_device(): jnp.einsum('rf,df->rd', hidden, down_t[i], preferred_element_type=jnp.flo...  19.3 us
    ppermute x2, starting transfers between devices, shift(): lax.ppermute(x, axis, [(i, i + distance) for i in range(n - distance)])  6.79 us
    slice x4, local copies, waits for them, and re-layouts, per_device(): got = swap(both[:, d * part:(d + 1) * part], 'rep', d)  5.2 us
  transfers between devices with their start and end apart: 33, of which 18 were waited for; matrix products, arithmetic and copies ran while one was open for 22% of the time, Pallas kernels for 0%

profile of v1, /device:TPU:0, one launch (start us, length us, event | category | flops | bytes accessed | tf_op | source)
XLA Modules:
  0.0 185.5 jit_solution(10615302946176326521)
XLA Ops:
  0.0 0.9 constant_dynamic-slice_fusion.1
  0.9 2.4 %collective-permute-start.3 = (bf16[128,256]{1,0:T(8,128)(2,1)S(1)}, bf16[128,256]{1,0:T(8,128)(2,1)S(1)}, u32[]{:S(2)}, u32[]{:S(2)}) collective-permute-start(bf16[128,256]{1,0:T(8,128)(2,1)S(1)} %pad_maximum_fusion.10), channel_id=1, source_target_pairs={{0,8},{8,16},{16,24},{1,9},{9,17},{17,25},{2,10},{10,18},{18,26},{... | collective-permute-start | bytes 196616 | tf_op jit(solution)/shard_map/ppermute | solution.py:23
  3.3 4.4 %collective-permute-start.2 = (bf16[128,256]{1,0:T(8,128)(2,1)S(1)}, bf16[128,256]{1,0:T(8,128)(2,1)S(1)}, u32[]{:S(2)}, u32[]{:S(2)}) collective-permute-start(bf16[128,256]{1,0:T(8,128)(2,1)S(1)} %pad_maximum_fusion.10), channel_id=1, source_target_pairs={{0,16},{8,24},{1,17},{9,25},{2,18},{10,26},{3,19},{11,27},{4,20},{... | collective-permute-start | bytes 196616 | tf_op jit(solution)/shard_map/ppermute | solution.py:23
  10.5 2.2 %collective-permute-done = f32[1,8,128]{2,1,0:T(8,128)S(1)} collective-permute-done((f32[1,8,128]{2,1,0:T(8,128)S(1)}, f32[1,8,128]{2,1,0:T(8,128)S(1)}, u32[]{:S(2)}, u32[]{:S(2)}) %collective-permute-start) | collective-permute-done | bytes 4128 | tf_op jit(solution)/shard_map/ppermute | solution.py:18
  14.1 1.2 reduce_window_sum.22
  17.7 1.6 collective-permute-start.6
  19.4 2.6 %collective-permute-start.9 = (bf16[128,768]{1,0:T(8,128)(2,1)S(1)}, bf16[128,768]{1,0:T(8,128)(2,1)S(1)}, u32[]{:S(2)}, u32[]{:S(2)}) collective-permute-start(bf16[128,768]{1,0:T(8,128)(2,1)S(1)} %copy.80), channel_id=1, source_target_pairs={{0,4},{2,6},{4,0},{6,2},{1,5},{3,7},{5,1},{7,3},{8,12},{10,14},{12... | collective-permute-start | bytes 589832 | tf_op jit(solution)/shard_map/ppermute | solution.py:18
  23.2 1.3 collective-permute-done.4
  24.7 3.7 %collective-permute-done.6 = bf16[128,768]{1,0:T(8,128)(2,1)S(1)} collective-permute-done((bf16[128,768]{1,0:T(8,128)(2,1)S(1)}, bf16[128,768]{1,0:T(8,128)(2,1)S(1)}, u32[]{:S(2)}, u32[]{:S(2)}) %collective-permute-start.6) | collective-permute-done | bytes 196640 | tf_op jit(solution)/shard_map/ppermute | solution.py:18
  28.4 1.6 collective-permute-start.7
  30.0 6.5 %collective-permute-done.9 = bf16[128,768]{1,0:T(8,128)(2,1)S(1)} collective-permute-done((bf16[128,768]{1,0:T(8,128)(2,1)S(1)}, bf16[128,768]{1,0:T(8,128)(2,1)S(1)}, u32[]{:S(2)}, u32[]{:S(2)}) %collective-permute-start.9) | collective-permute-done | bytes 196640 | tf_op jit(solution)/shard_map/ppermute | solution.py:18
  36.5 2.0 %collective-permute-start.10 = (bf16[1,1,128,768]{3,2,1,0:T(8,128)(2,1)S(1)}, bf16[1,1,128,768]{3,2,1,0:T(8,128)(2,1)S(1)}, u32[]{:S(2)}, u32[]{:S(2)}) collective-permute-start(bf16[1,1,128,768]{3,2,1,0:T(8,128)(2,1)S(1)} %bitcast.341), channel_id=1, source_target_pairs={{0,16},{8,24},{16,0},{24,8},{1,17},{9,25},{17,1},{25,9},{2,18},{10... | collective-permute-start | bytes 589832 | tf_op jit(solution)/shard_map/ppermute | solution.py:18
  38.5 1.0 fusion.70
  39.7 2.5 %collective-permute-done.10 = bf16[1,1,128,768]{3,2,1,0:T(8,128)(2,1)S(1)} collective-permute-done((bf16[1,1,128,768]{3,2,1,0:T(8,128)(2,1)S(1)}, bf16[1,1,128,768]{3,2,1,0:T(8,128)(2,1)S(1)}, u32[]{:S(2)}, u32[]{:S(2)}) %collective-permute-start.10) | collective-permute-done | bytes 196640 | tf_op jit(solution)/shard_map/ppermute | solution.py:18
  42.3 2.9 %collective-permute-done.13 = bf16[1,1,128,768]{3,2,1,0:T(8,128)(2,1)S(1)} collective-permute-done((bf16[1,1,128,768]{3,2,1,0:T(8,128)(2,1)S(1)}, bf16[1,1,128,768]{3,2,1,0:T(8,128)(2,1)S(1)}, u32[]{:S(2)}, u32[]{:S(2)}) %collective-permute-start.13) | collective-permute-done | bytes 196640 | tf_op jit(solution)/shard_map/ppermute | solution.py:18
  46.1 0.9 collective-permute-done.14
  47.5 10.8 %fusion.52 = bf16[2,136,1344]{2,1,0:T(8,128)(2,1)} fusion(bf16[4,3072,2,1344]{1,3,2,0:T(8,128)(2,1)} %param.14, bf16[512,3072]{1,0:T(8,128)(2,1)S(1)} %bitcast.325, pred[4,136,512]{2,1,0:T(8,128)(4,1)S(1)} %broadcast_compare_fusion), kind=kOutput, calls=%fused_computation.45 | convolution fusion | flops 2674652160 | bytes 20461568 | tf_op jit(solution)/shard_map/rd,dgf->grf/dot_general | solution.py:146
  58.3 10.8 %fusion.55 = bf16[2,136,1344]{2,1,0:T(8,128)(2,1)} fusion(bf16[4,3072,2,1344]{1,3,2,0:T(8,128)(2,1)} %param.14, bf16[512,3072]{1,0:T(8,128)(2,1)S(1)} %bitcast.326, pred[4,136,512]{2,1,0:T(8,128)(4,1)S(1)} %broadcast_compare_fusion), kind=kOutput, calls=%fused_computation.46 | convolution fusion | flops 2674652160 | bytes 20461568 | tf_op jit(solution)/shard_map/rd,dgf->grf/dot_general | solution.py:146
  69.1 10.8 %fusion.58 = bf16[2,136,1344]{2,1,0:T(8,128)(2,1)} fusion(bf16[4,3072,2,1344]{1,3,2,0:T(8,128)(2,1)} %param.14, bf16[512,3072]{1,0:T(8,128)(2,1)S(1)} %bitcast.327, pred[4,136,512]{2,1,0:T(8,128)(4,1)S(1)} %broadcast_compare_fusion), kind=kOutput, calls=%fused_computation.47 | convolution fusion | flops 2674652160 | bytes 20461568 | tf_op jit(solution)/shard_map/rd,dgf->grf/dot_general | solution.py:146
  79.9 1.8 slice.233
  81.7 1.5 collective-permute-start.21
  83.2 10.8 %fusion.61 = bf16[2,136,1344]{2,1,0:T(8,128)(2,1)} fusion(bf16[4,3072,2,1344]{1,3,2,0:T(8,128)(2,1)} %param.14, bf16[512,3072]{1,0:T(8,128)(2,1)S(1)} %bitcast.328, pred[4,136,512]{2,1,0:T(8,128)(4,1)} %copy-done.6), kind=kOutput, calls=%fused_computation.48 | convolution fusion | flops 2674652160 | bytes 20461568 | tf_op jit(solution)/shard_map/rd,dgf->grf/dot_general | solution.py:146
  94.0 1.2 slice.228
  95.8 1.1 slice.223
  96.9 1.6 collective-permute-start.17
  98.5 1.1 slice.218
  100.2 1.1 convert_add_fusion.2
  101.4 1.6 collective-permute-start.22
  103.0 4.6 %collective-permute-done.19 = bf16[2,68,1344]{2,1,0:T(8,128)(2,1)S(1)} collective-permute-done((bf16[2,68,1344]{2,1,0:T(8,128)(2,1)S(1)}, bf16[2,68,1344]{2,1,0:T(8,128)(2,1)S(1)}, u32[]{:S(2)}, u32[]{:S(2)}) %collective-permute-start.19) | collective-permute-done | bytes 365600 | tf_op jit(solution)/shard_map/ppermute | solution.py:18
  108.3 7.9 %collective-permute-done.17 = bf16[2,68,1344]{2,1,0:T(8,128)(2,1)S(1)} collective-permute-done((bf16[2,68,1344]{2,1,0:T(8,128)(2,1)S(1)}, bf16[2,68,1344]{2,1,0:T(8,128)(2,1)S(1)}, u32[]{:S(2)}, u32[]{:S(2)}) %collective-permute-start.17) | collective-permute-done | bytes 365600 | tf_op jit(solution)/shard_map/ppermute | solution.py:18
  117.0 7.9 %collective-permute-done.15 = bf16[2,68,1344]{2,1,0:T(8,128)(2,1)S(1)} collective-permute-done((bf16[2,68,1344]{2,1,0:T(8,128)(2,1)S(1)}, bf16[2,68,1344]{2,1,0:T(8,128)(2,1)S(1)}, u32[]{:S(2)}, u32[]{:S(2)}) %collective-permute-start.15) | collective-permute-done | bytes 365600 | tf_op jit(solution)/shard_map/ppermute | solution.py:18
  125.7 3.5 %collective-permute-done.22 = bf16[68,1344]{1,0:T(8,128)(2,1)S(1)} collective-permute-done((bf16[68,1344]{1,0:T(8,128)(2,1)S(1)}, bf16[68,1344]{1,0:T(8,128)(2,1)S(1)}, u32[]{:S(2)}, u32[]{:S(2)}) %collective-permute-start.22) | collective-permute-done | bytes 182816 | tf_op jit(solution)/shard_map/ppermute | solution.py:18
  129.3 4.8 %fusion.33 = bf16[136,3072]{1,0:T(8,128)(2,1)S(1)} fusion(bf16[4,3072,1344]{1,2,0:T(8,128)(2,1)} %param.15, bf16[68,1344]{1,0:T(8,128)(2,1)S(1)} %collective-permute-done.22, bf16[68,1344]{1,0:T(8,128)(2,1)S(1)} %fusion.78), kind=kOutput, calls=%fused_computation.29 | convolution fusion | flops 1124173824 | bytes 9458688 | tf_op jit(solution)/shard_map/rf,df->rd/dot_general | solution.py:154
  134.1 4.8 %fusion.30 = bf16[136,3072]{1,0:T(8,128)(2,1)S(1)} fusion(bf16[4,3072,1344]{1,2,0:T(8,128)(2,1)} %param.15, bf16[68,1344]{1,0:T(8,128)(2,1)S(1)} %collective-permute-done.20, bf16[68,1344]{1,0:T(8,128)(2,1)S(1)} %fusion.80), kind=kOutput, calls=%fused_computation.28 | convolution fusion | flops 1124173824 | bytes 9458688 | tf_op jit(solution)/shard_map/rf,df->rd/dot_general | solution.py:154
  139.0 4.8 %fusion.27 = bf16[136,3072]{1,0:T(8,128)(2,1)S(1)} fusion(bf16[4,3072,1344]{1,2,0:T(8,128)(2,1)} %param.15, bf16[68,1344]{1,0:T(8,128)(2,1)S(1)} %collective-permute-done.18, bf16[68,1344]{1,0:T(8,128)(2,1)S(1)} %fusion.82), kind=kOutput, calls=%fused_computation.27 | convolution fusion | flops 1124173824 | bytes 9458688 | tf_op jit(solution)/shard_map/rf,df->rd/dot_general | solution.py:154
  143.8 4.8 %fusion.24 = bf16[136,3072]{1,0:T(8,128)(2,1)S(1)} fusion(bf16[4,3072,1344]{1,2,0:T(8,128)(2,1)} %param.15, bf16[68,1344]{1,0:T(8,128)(2,1)S(1)} %collective-permute-done.16, bf16[68,1344]{1,0:T(8,128)(2,1)S(1)} %fusion.84), kind=kOutput, calls=%fused_computation.26 | convolution fusion | flops 1124173824 | bytes 9458688 | tf_op jit(solution)/shard_map/rf,df->rd/dot_general | solution.py:154
  149.7 1.4 convolution_convert_fusion.4
  151.3 1.4 convolution_convert_fusion.5
  153.8 1.2 collective-permute-start.29
  155.5 1.2 collective-permute-start.24
  156.7 9.2 %collective-permute-done.29 = bf16[1,128,1536]{2,1,0:T(8,128)(2,1)S(1)} collective-permute-done((bf16[1,128,1536]{2,1,0:T(8,128)(2,1)S(1)}, bf16[1,128,1536]{2,1,0:T(8,128)(2,1)S(1)}, u32[]{:S(2)}, u32[]{:S(2)}) %collective-permute-start.29) | collective-permute-done | bytes 393248 | tf_op jit(solution)/shard_map/ppermute | solution.py:18
  165.9 2.9 %collective-permute-start.32 = (bf16[32,1536]{1,0:T(8,128)(2,1)S(1)}, bf16[32,1536]{1,0:T(8,128)(2,1)S(1)}, u32[]{:S(2)}, u32[]{:S(2)}) collective-permute-start(bf16[32,1536]{1,0:T(8,128)(2,1)S(1)} %get-tuple-element.9), channel_id=1, source_target_pairs={{0,6},{2,4},{4,2},{6,0},{1,7},{3,5},{5,3},{7,1},{8,14},{10,12},{12... | collective-permute-start | bytes 294920 | tf_op jit(solution)/shard_map/ppermute | solution.py:18
  168.8 1.6 collective-permute-start.30
  170.4 3.0 %collective-permute-done.24 = bf16[1,128,1536]{2,1,0:T(8,128)(2,1)S(1)} collective-permute-done((bf16[1,128,1536]{2,1,0:T(8,128)(2,1)S(1)}, bf16[1,128,1536]{2,1,0:T(8,128)(2,1)S(1)}, u32[]{:S(2)}, u32[]{:S(2)}) %collective-permute-start.24) | collective-permute-done | bytes 393248 | tf_op jit(solution)/shard_map/ppermute | solution.py:18
  173.6 2.9 %collective-permute-start.27 = (bf16[32,1536]{1,0:T(8,128)(2,1)S(1)}, bf16[32,1536]{1,0:T(8,128)(2,1)S(1)}, u32[]{:S(2)}, u32[]{:S(2)}) collective-permute-start(bf16[32,1536]{1,0:T(8,128)(2,1)S(1)} %get-tuple-element.6), channel_id=1, source_target_pairs={{0,6},{2,4},{4,2},{6,0},{1,7},{3,5},{5,3},{7,1},{8,14},{10,12},{12... | collective-permute-start | bytes 294920 | tf_op jit(solution)/shard_map/ppermute | solution.py:18
  176.4 1.6 collective-permute-start.25
  178.1 2.8 %collective-permute-done.27 = bf16[32,1536]{1,0:T(8,128)(2,1)S(1)} collective-permute-done((bf16[32,1536]{1,0:T(8,128)(2,1)S(1)}, bf16[32,1536]{1,0:T(8,128)(2,1)S(1)}, u32[]{:S(2)}, u32[]{:S(2)}) %collective-permute-start.27) | collective-permute-done | bytes 98336 | tf_op jit(solution)/shard_map/ppermute | solution.py:18
  180.9 3.8 %collective-permute-done.26 = bf16[32,1536]{1,0:T(8,128)(2,1)S(1)} collective-permute-done((bf16[32,1536]{1,0:T(8,128)(2,1)S(1)}, bf16[32,1536]{1,0:T(8,128)(2,1)S(1)}, u32[]{:S(2)}, u32[]{:S(2)}) %collective-permute-start.26) | collective-permute-done | bytes 98336 | tf_op jit(solution)/shard_map/ppermute | solution.py:18
  (135 shorter events, 16.7 us)
Async XLA Ops:
  0.0 10.3 %copy-start = (bf16[128,6144]{1,0:T(8,128)(2,1)S(1)}, bf16[128,6144]{1,0:T(8,128)(2,1)}, u32[]{:S(2)}) copy-start(bf16[128,6144]{1,0:T(8,128)(2,1)} %param.8) | copy-start | bytes 4718596
  0.9 15.5 %collective-permute-start.3 = (bf16[128,256]{1,0:T(8,128)(2,1)S(1)}, bf16[128,256]{1,0:T(8,128)(2,1)S(1)}, u32[]{:S(2)}, u32[]{:S(2)}) collective-permute-start(bf16[128,256]{1,0:T(8,128)(2,1)S(1)} %pad_maximum_fusion.10), channel_id=1, source_target_pairs={{0,8},{8,16},{16,24},{1,9},{9,17},{17,25},{2,10},{10,18},{18,26},{... | collective-permute-start | bytes 196616 | tf_op jit(solution)/shard_map/ppermute | solution.py:23
  3.3 13.2 %collective-permute-start.2 = (bf16[128,256]{1,0:T(8,128)(2,1)S(1)}, bf16[128,256]{1,0:T(8,128)(2,1)S(1)}, u32[]{:S(2)}, u32[]{:S(2)}) collective-permute-start(bf16[128,256]{1,0:T(8,128)(2,1)S(1)} %pad_maximum_fusion.10), channel_id=1, source_target_pairs={{0,16},{8,24},{1,17},{9,25},{2,18},{10,26},{3,19},{11,27},{4,20},{... | collective-permute-start | bytes 196616 | tf_op jit(solution)/shard_map/ppermute | solution.py:23
  9.1 3.6 %collective-permute-start = (f32[1,8,128]{2,1,0:T(8,128)S(1)}, f32[1,8,128]{2,1,0:T(8,128)S(1)}, u32[]{:S(2)}, u32[]{:S(2)}) collective-permute-start(f32[1,8,128]{2,1,0:T(8,128)S(1)} %get-tuple-element.24), channel_id=1, source_target_pairs={{0,16},{8,24},{16,0},{24,8},{1,17},{9,25},{17,1},{25,9},{2,18},{10... | collective-permute-start | bytes 12296 | tf_op jit(solution)/shard_map/ppermute | solution.py:18
  12.7 1.2 collective-permute-start.1
  15.6 53.4 %copy-start.6 = (pred[4,136,512]{2,1,0:T(8,128)(4,1)}, pred[4,136,512]{2,1,0:T(8,128)(4,1)S(1)}, u32[]{:S(2)}) copy-start(pred[4,136,512]{2,1,0:T(8,128)(4,1)S(1)} %broadcast_compare_fusion) | copy-start | bytes 835588
  17.5 7.0 %collective-permute-start.4 = (bf16[1,1,128,768]{3,2,1,0:T(8,128)(2,1)S(1)}, bf16[1,1,128,768]{3,2,1,0:T(8,128)(2,1)S(1)}, u32[]{:S(2)}, u32[]{:S(2)}) collective-permute-start(bf16[1,1,128,768]{3,2,1,0:T(8,128)(2,1)S(1)} %copy.77), channel_id=1, source_target_pairs={{0,16},{8,24},{16,0},{24,8},{1,17},{9,25},{17,1},{25,9},{2,18},{10... | collective-permute-start | bytes 589832 | tf_op jit(solution)/shard_map/ppermute | solution.py:18
  17.7 10.7 %collective-permute-start.6 = (bf16[128,768]{1,0:T(8,128)(2,1)S(1)}, bf16[128,768]{1,0:T(8,128)(2,1)S(1)}, u32[]{:S(2)}, u32[]{:S(2)}) collective-permute-start(bf16[128,768]{1,0:T(8,128)(2,1)S(1)} %copy.80), channel_id=1, source_target_pairs={{0,2},{2,0},{4,6},{6,4},{1,3},{3,1},{5,7},{7,5},{8,10},{10,8},{12,... | collective-permute-start | bytes 589832 | tf_op jit(solution)/shard_map/ppermute | solution.py:18
  19.4 17.1 %collective-permute-start.9 = (bf16[128,768]{1,0:T(8,128)(2,1)S(1)}, bf16[128,768]{1,0:T(8,128)(2,1)S(1)}, u32[]{:S(2)}, u32[]{:S(2)}) collective-permute-start(bf16[128,768]{1,0:T(8,128)(2,1)S(1)} %copy.80), channel_id=1, source_target_pairs={{0,4},{2,6},{4,0},{6,2},{1,5},{3,7},{5,1},{7,3},{8,12},{10,14},{12... | collective-permute-start | bytes 589832 | tf_op jit(solution)/shard_map/ppermute | solution.py:18
  22.9 16.7 %collective-permute-start.12 = (bf16[128,768]{1,0:T(8,128)(2,1)S(1)}, bf16[128,768]{1,0:T(8,128)(2,1)S(1)}, u32[]{:S(2)}, u32[]{:S(2)}) collective-permute-start(bf16[128,768]{1,0:T(8,128)(2,1)S(1)} %copy.80), channel_id=1, source_target_pairs={{0,6},{2,4},{4,2},{6,0},{1,7},{3,5},{5,3},{7,1},{8,14},{10,12},{12... | collective-permute-start | bytes 589832 | tf_op jit(solution)/shard_map/ppermute | solution.py:18
  24.6 20.8 %collective-permute-start.5 = (bf16[2,1,128,768]{3,2,0,1:T(8,128)(2,1)S(1)}, bf16[2,1,128,768]{3,2,0,1:T(8,128)(2,1)S(1)}, u32[]{:S(2)}, u32[]{:S(2)}) collective-permute-start(bf16[2,1,128,768]{3,2,0,1:T(8,128)(2,1)S(1)} %get-tuple-element.18), channel_id=1, source_target_pairs={{0,8},{8,0},{16,24},{24,16},{1,9},{9,1},{17,25},{25,17},{2,10},{10... | collective-permute-start | bytes 1179656 | tf_op jit(solution)/shard_map/ppermute | solution.py:18
  28.4 11.1 %collective-permute-start.7 = (bf16[1,1,128,768]{3,2,1,0:T(8,128)(2,1)S(1)}, bf16[1,1,128,768]{3,2,1,0:T(8,128)(2,1)S(1)}, u32[]{:S(2)}, u32[]{:S(2)}) collective-permute-start(bf16[1,1,128,768]{3,2,1,0:T(8,128)(2,1)S(1)} %bitcast.343), channel_id=1, source_target_pairs={{0,16},{8,24},{16,0},{24,8},{1,17},{9,25},{17,1},{25,9},{2,18},{10... | collective-permute-start | bytes 589832 | tf_op jit(solution)/shard_map/ppermute | solution.py:18
  36.5 5.7 %collective-permute-start.10 = (bf16[1,1,128,768]{3,2,1,0:T(8,128)(2,1)S(1)}, bf16[1,1,128,768]{3,2,1,0:T(8,128)(2,1)S(1)}, u32[]{:S(2)}, u32[]{:S(2)}) collective-permute-start(bf16[1,1,128,768]{3,2,1,0:T(8,128)(2,1)S(1)} %bitcast.341), channel_id=1, source_target_pairs={{0,16},{8,24},{16,0},{24,8},{1,17},{9,25},{17,1},{25,9},{2,18},{10... | collective-permute-start | bytes 589832 | tf_op jit(solution)/shard_map/ppermute | solution.py:18
  39.5 5.7 %collective-permute-start.13 = (bf16[1,1,128,768]{3,2,1,0:T(8,128)(2,1)S(1)}, bf16[1,1,128,768]{3,2,1,0:T(8,128)(2,1)S(1)}, u32[]{:S(2)}, u32[]{:S(2)}) collective-permute-start(bf16[1,1,128,768]{3,2,1,0:T(8,128)(2,1)S(1)} %bitcast.345), channel_id=1, source_target_pairs={{0,16},{8,24},{16,0},{24,8},{1,17},{9,25},{17,1},{25,9},{2,18},{10... | collective-permute-start | bytes 589832 | tf_op jit(solution)/shard_map/ppermute | solution.py:18
  39.6 6.3 %collective-permute-start.8 = (bf16[2,1,128,768]{3,2,0,1:T(8,128)(2,1)S(1)}, bf16[2,1,128,768]{3,2,0,1:T(8,128)(2,1)S(1)}, u32[]{:S(2)}, u32[]{:S(2)}) collective-permute-start(bf16[2,1,128,768]{3,2,0,1:T(8,128)(2,1)S(1)} %get-tuple-element.16), channel_id=1, source_target_pairs={{0,8},{8,0},{16,24},{24,16},{1,9},{9,1},{17,25},{25,17},{2,10},{10... | collective-permute-start | bytes 1179656 | tf_op jit(solution)/shard_map/ppermute | solution.py:18
  42.2 3.8 %collective-permute-start.11 = (bf16[2,1,128,768]{3,2,0,1:T(8,128)(2,1)S(1)}, bf16[2,1,128,768]{3,2,0,1:T(8,128)(2,1)S(1)}, u32[]{:S(2)}, u32[]{:S(2)}) collective-permute-start(bf16[2,1,128,768]{3,2,0,1:T(8,128)(2,1)S(1)} %get-tuple-element.14), channel_id=1, source_target_pairs={{0,8},{8,0},{16,24},{24,16},{1,9},{9,1},{17,25},{25,17},{2,10},{10... | collective-permute-start | bytes 1179656 | tf_op jit(solution)/shard_map/ppermute | solution.py:18
  45.3 1.8 collective-permute-start.14
  81.7 18.4 %collective-permute-start.21 = (bf16[2,68,1344]{2,1,0:T(8,128)(2,1)}, bf16[2,68,1344]{2,1,0:T(8,128)(2,1)S(1)}, u32[]{:S(2)}, u32[]{:S(2)}) collective-permute-start(bf16[2,68,1344]{2,1,0:T(8,128)(2,1)} %slice.233), channel_id=1, source_target_pairs={{0,1},{1,0},{2,3},{3,2},{4,5},{5,4},{6,7},{7,6},{8,9},{9,8},{10,11... | collective-permute-start | bytes 1096712 | tf_op jit(solution)/shard_map/ppermute | solution.py:18
  94.0 13.5 %copy-start.4 = (bf16[2,136,1344]{2,1,0:T(8,128)(2,1)S(1)}, bf16[2,136,1344]{2,1,0:T(8,128)(2,1)}, u32[]{:S(2)}) copy-start(bf16[2,136,1344]{2,1,0:T(8,128)(2,1)} %fusion.55) | copy-start | bytes 2193412
  95.2 12.3 %collective-permute-start.19 = (bf16[2,68,1344]{2,1,0:T(8,128)(2,1)S(1)}, bf16[2,68,1344]{2,1,0:T(8,128)(2,1)S(1)}, u32[]{:S(2)}, u32[]{:S(2)}) collective-permute-start(bf16[2,68,1344]{2,1,0:T(8,128)(2,1)S(1)} %slice.228), channel_id=1, source_target_pairs={{0,1},{1,0},{2,3},{3,2},{4,5},{5,4},{6,7},{7,6},{8,9},{9,8},{10,11... | collective-permute-start | bytes 1096712 | tf_op jit(solution)/shard_map/ppermute | solution.py:18
  96.9 19.3 %copy-start.3 = (bf16[2,136,1344]{2,1,0:T(8,128)(2,1)S(1)}, bf16[2,136,1344]{2,1,0:T(8,128)(2,1)}, u32[]{:S(2)}) copy-start(bf16[2,136,1344]{2,1,0:T(8,128)(2,1)} %fusion.58) | copy-start | bytes 2193412
  96.9 19.3 %collective-permute-start.17 = (bf16[2,68,1344]{2,1,0:T(8,128)(2,1)S(1)}, bf16[2,68,1344]{2,1,0:T(8,128)(2,1)S(1)}, u32[]{:S(2)}, u32[]{:S(2)}) collective-permute-start(bf16[2,68,1344]{2,1,0:T(8,128)(2,1)S(1)} %slice.223), channel_id=1, source_target_pairs={{0,1},{1,0},{2,3},{3,2},{4,5},{5,4},{6,7},{7,6},{8,9},{9,8},{10,11... | collective-permute-start | bytes 1096712 | tf_op jit(solution)/shard_map/ppermute | solution.py:18
  99.6 25.3 %collective-permute-start.15 = (bf16[2,68,1344]{2,1,0:T(8,128)(2,1)S(1)}, bf16[2,68,1344]{2,1,0:T(8,128)(2,1)S(1)}, u32[]{:S(2)}, u32[]{:S(2)}) collective-permute-start(bf16[2,68,1344]{2,1,0:T(8,128)(2,1)S(1)} %slice.218), channel_id=1, source_target_pairs={{0,1},{1,0},{2,3},{3,2},{4,5},{5,4},{6,7},{7,6},{8,9},{9,8},{10,11... | collective-permute-start | bytes 1096712 | tf_op jit(solution)/shard_map/ppermute | solution.py:18
  101.3 23.7 %copy-start.2 = (bf16[2,136,1344]{2,1,0:T(8,128)(2,1)S(1)}, bf16[2,136,1344]{2,1,0:T(8,128)(2,1)}, u32[]{:S(2)}) copy-start(bf16[2,136,1344]{2,1,0:T(8,128)(2,1)} %fusion.61) | copy-start | bytes 2193412
  101.4 27.9 %collective-permute-start.22 = (bf16[68,1344]{1,0:T(8,128)(2,1)S(1)}, bf16[68,1344]{1,0:T(8,128)(2,1)S(1)}, u32[]{:S(2)}, u32[]{:S(2)}) collective-permute-start(bf16[68,1344]{1,0:T(8,128)(2,1)S(1)} %fusion.78), channel_id=1, source_target_pairs={{0,1},{1,0},{2,3},{3,2},{4,5},{5,4},{6,7},{7,6},{8,9},{9,8},{10,11... | collective-permute-start | bytes 548360 | tf_op jit(solution)/shard_map/ppermute | solution.py:18
  107.8 26.4 %collective-permute-start.20 = (bf16[68,1344]{1,0:T(8,128)(2,1)S(1)}, bf16[68,1344]{1,0:T(8,128)(2,1)S(1)}, u32[]{:S(2)}, u32[]{:S(2)}) collective-permute-start(bf16[68,1344]{1,0:T(8,128)(2,1)S(1)} %fusion.80), channel_id=1, source_target_pairs={{0,1},{1,0},{2,3},{3,2},{4,5},{5,4},{6,7},{7,6},{8,9},{9,8},{10,11... | collective-permute-start | bytes 548360 | tf_op jit(solution)/shard_map/ppermute | solution.py:18
  116.4 22.5 %collective-permute-start.18 = (bf16[68,1344]{1,0:T(8,128)(2,1)S(1)}, bf16[68,1344]{1,0:T(8,128)(2,1)S(1)}, u32[]{:S(2)}, u32[]{:S(2)}) collective-permute-start(bf16[68,1344]{1,0:T(8,128)(2,1)S(1)} %fusion.82), channel_id=1, source_target_pairs={{0,1},{1,0},{2,3},{3,2},{4,5},{5,4},{6,7},{7,6},{8,9},{9,8},{10,11... | collective-permute-start | bytes 548360 | tf_op jit(solution)/shard_map/ppermute | solution.py:18
  125.1 18.7 %collective-permute-start.16 = (bf16[68,1344]{1,0:T(8,128)(2,1)S(1)}, bf16[68,1344]{1,0:T(8,128)(2,1)S(1)}, u32[]{:S(2)}, u32[]{:S(2)}) collective-permute-start(bf16[68,1344]{1,0:T(8,128)(2,1)S(1)} %fusion.84), channel_id=1, source_target_pairs={{0,1},{1,0},{2,3},{3,2},{4,5},{5,4},{6,7},{7,6},{8,9},{9,8},{10,11... | collective-permute-start | bytes 548360 | tf_op jit(solution)/shard_map/ppermute | solution.py:18
  148.7 1.1 copy-start.5
  151.2 2.4 %collective-permute-start.28 = (bf16[2,128,1536]{2,1,0:T(8,128)(2,1)S(1)}, bf16[2,128,1536]{2,1,0:T(8,128)(2,1)S(1)}, u32[]{:S(2)}, u32[]{:S(2)}) collective-permute-start(bf16[2,128,1536]{2,1,0:T(8,128)(2,1)S(1)} %slice_bitcast_fusion), channel_id=1, source_target_pairs={{0,8},{8,0},{16,24},{24,16},{1,9},{9,1},{17,25},{25,17},{2,10},{10... | collective-permute-start | bytes 2359304 | tf_op jit(solution)/shard_map/ppermute | solution.py:18
  152.8 2.5 %collective-permute-start.23 = (bf16[2,128,1536]{2,1,0:T(8,128)(2,1)S(1)}, bf16[2,128,1536]{2,1,0:T(8,128)(2,1)S(1)}, u32[]{:S(2)}, u32[]{:S(2)}) collective-permute-start(bf16[2,128,1536]{2,1,0:T(8,128)(2,1)S(1)} %slice_bitcast_fusion.2), channel_id=1, source_target_pairs={{0,8},{8,0},{16,24},{24,16},{1,9},{9,1},{17,25},{25,17},{2,10},{10... | collective-permute-start | bytes 2359304 | tf_op jit(solution)/shard_map/ppermute | solution.py:18
  153.8 12.0 %collective-permute-start.29 = (bf16[1,128,1536]{2,1,0:T(8,128)(2,1)S(1)}, bf16[1,128,1536]{2,1,0:T(8,128)(2,1)S(1)}, u32[]{:S(2)}, u32[]{:S(2)}) collective-permute-start(bf16[1,128,1536]{2,1,0:T(8,128)(2,1)S(1)} %slice_bitcast_fusion.12), channel_id=1, source_target_pairs={{0,16},{8,24},{16,0},{24,8},{1,17},{9,25},{17,1},{25,9},{2,18},{10... | collective-permute-start | bytes 1179656 | tf_op jit(solution)/shard_map/ppermute | solution.py:18
  155.2 30.3 %copy-start.1 = (bf16[128,6144]{1,0:T(8,128)(2,1)S(1)}, bf16[128,6144]{1,0:T(8,128)(2,1)}, u32[]{:S(2)}) copy-start(bf16[128,6144]{1,0:T(8,128)(2,1)} %param.8) | copy-start | bytes 4718596
  155.5 18.0 %collective-permute-start.24 = (bf16[1,128,1536]{2,1,0:T(8,128)(2,1)S(1)}, bf16[1,128,1536]{2,1,0:T(8,128)(2,1)S(1)}, u32[]{:S(2)}, u32[]{:S(2)}) collective-permute-start(bf16[1,128,1536]{2,1,0:T(8,128)(2,1)S(1)} %slice_bitcast_fusion.14), channel_id=1, source_target_pairs={{0,16},{8,24},{16,0},{24,8},{1,17},{9,25},{17,1},{25,9},{2,18},{10... | collective-permute-start | bytes 1179656 | tf_op jit(solution)/shard_map/ppermute | solution.py:18
  165.9 10.5 %collective-permute-start.32 = (bf16[32,1536]{1,0:T(8,128)(2,1)S(1)}, bf16[32,1536]{1,0:T(8,128)(2,1)S(1)}, u32[]{:S(2)}, u32[]{:S(2)}) collective-permute-start(bf16[32,1536]{1,0:T(8,128)(2,1)S(1)} %get-tuple-element.9), channel_id=1, source_target_pairs={{0,6},{2,4},{4,2},{6,0},{1,7},{3,5},{5,3},{7,1},{8,14},{10,12},{12... | collective-permute-start | bytes 294920 | tf_op jit(solution)/shard_map/ppermute | solution.py:18
  168.8 9.2 %collective-permute-start.31 = (bf16[32,1536]{1,0:T(8,128)(2,1)S(1)}, bf16[32,1536]{1,0:T(8,128)(2,1)S(1)}, u32[]{:S(2)}, u32[]{:S(2)}) collective-permute-start(bf16[32,1536]{1,0:T(8,128)(2,1)S(1)} %get-tuple-element.10), channel_id=1, source_target_pairs={{0,4},{2,6},{4,0},{6,2},{1,5},{3,7},{5,1},{7,3},{8,12},{10,14},{12... | collective-permute-start | bytes 294920 | tf_op jit(solution)/shard_map/ppermute | solution.py:18
  168.8 9.2 %collective-permute-start.30 = (bf16[32,1536]{1,0:T(8,128)(2,1)S(1)}, bf16[32,1536]{1,0:T(8,128)(2,1)S(1)}, u32[]{:S(2)}, u32[]{:S(2)}) collective-permute-start(bf16[32,1536]{1,0:T(8,128)(2,1)S(1)} %get-tuple-element.8), channel_id=1, source_target_pairs={{0,2},{2,0},{4,6},{6,4},{1,3},{3,1},{5,7},{7,5},{8,10},{10,8},{12,... | collective-permute-start | bytes 294920 | tf_op jit(solution)/shard_map/ppermute | solution.py:18
  173.6 7.4 %collective-permute-start.27 = (bf16[32,1536]{1,0:T(8,128)(2,1)S(1)}, bf16[32,1536]{1,0:T(8,128)(2,1)S(1)}, u32[]{:S(2)}, u32[]{:S(2)}) collective-permute-start(bf16[32,1536]{1,0:T(8,128)(2,1)S(1)} %get-tuple-element.6), channel_id=1, source_target_pairs={{0,6},{2,4},{4,2},{6,0},{1,7},{3,5},{5,3},{7,1},{8,14},{10,12},{12... | collective-permute-start | bytes 294920 | tf_op jit(solution)/shard_map/ppermute | solution.py:18
  176.4 8.3 %collective-permute-start.26 = (bf16[32,1536]{1,0:T(8,128)(2,1)S(1)}, bf16[32,1536]{1,0:T(8,128)(2,1)S(1)}, u32[]{:S(2)}, u32[]{:S(2)}) collective-permute-start(bf16[32,1536]{1,0:T(8,128)(2,1)S(1)} %get-tuple-element.7), channel_id=1, source_target_pairs={{0,4},{2,6},{4,0},{6,2},{1,5},{3,7},{5,1},{7,3},{8,12},{10,14},{12... | collective-permute-start | bytes 294920 | tf_op jit(solution)/shard_map/ppermute | solution.py:18
  176.4 8.3 %collective-permute-start.25 = (bf16[32,1536]{1,0:T(8,128)(2,1)S(1)}, bf16[32,1536]{1,0:T(8,128)(2,1)S(1)}, u32[]{:S(2)}, u32[]{:S(2)}) collective-permute-start(bf16[32,1536]{1,0:T(8,128)(2,1)S(1)} %get-tuple-element.5), channel_id=1, source_target_pairs={{0,2},{2,0},{4,6},{6,4},{1,3},{3,1},{5,7},{7,5},{8,10},{10,8},{12,... | collective-permute-start | bytes 294920 | tf_op jit(solution)/shard_map/ppermute | solution.py:18

commit v2 on v1

--- a/solution.py
+++ b/solution.py
@@ -1,6 +1,8 @@
 import jax
 import jax.numpy as jnp
 from jax import lax
+from jax.experimental import pallas as pl
+from jax.experimental.pallas import tpu as pltpu
 from jax.sharding import PartitionSpec as P
 
 HEADS = 48
@@ -11,6 +13,9 @@
 CAP = 34
 GROUP = HEADS // KV
 TAIL_PIECES = 2
+SLOTS = 4
+F_STEP = 384
+D_STEP = 512
 
 
 def swap(x, axis, distance):
@@ -98,6 +103,156 @@
     return full.reshape(n_seq * tok, cols)
 
 
+def expert_kernel(p_ref, wg_ref, wd_ref, out_ref, wbuf, kept, sent, got, hid, wsem, s1, r1, s2, r2):
+    r = lax.axis_index("rep")
+    partner = {"rep": 1 - r}
+    owned, rows, cols = out_ref.shape
+    hidden = wbuf.shape[1]
+    pairs = owned // 2
+    mine = [2 * p + r for p in range(pairs)]
+    theirs = [2 * p + 1 - r for p in range(pairs)]
+    blocks = [wg_ref.at[2 * e + g] for e in theirs + mine for g in range(2)]
+    blocks += [wd_ref.at[e] for e in mine + theirs]
+
+    def load(t):
+        return pltpu.make_async_copy(blocks[t], wbuf.at[t % SLOTS], wsem.at[t % SLOTS])
+
+    for t in range(SLOTS):
+        load(t).start()
+    barrier = pltpu.get_barrier_semaphore()
+    pl.semaphore_signal(barrier, inc=1, device_id=partner, device_id_type=pl.DeviceIdType.MESH)
+    pl.semaphore_wait(barrier, 1)
+
+    def refill(t):
+        if t + SLOTS < len(blocks):
+            load(t + SLOTS).start()
+
+    def gate_part(t, e, dst):
+        load(t).wait()
+        w = wbuf.at[t % SLOTS]
+
+        def piece(start, size):
+            acc = lax.dot_general(
+                w[pl.ds(start, size), :],
+                p_ref[e],
+                (((1,), (1,)), ((), ())),
+                preferred_element_type=jnp.float32,
+            )
+            dst[:, pl.ds(start, size)] = acc.T.astype(jnp.bfloat16)
+
+        whole = hidden // F_STEP
+
+        @pl.loop(0, whole)
+        def _(k):
+            piece(pl.multiple_of(k * F_STEP, F_STEP), F_STEP)
+
+        if hidden % F_STEP:
+            piece(whole * F_STEP, hidden % F_STEP)
+        refill(t)
+
+    def reduce_copy(p, g):
+        return pltpu.make_async_remote_copy(
+            src_ref=sent.at[p, g],
+            dst_ref=got.at[p, g],
+            send_sem=s1.at[p, g],
+            recv_sem=r1.at[p, g],
+            device_id=partner,
+            device_id_type=pl.DeviceIdType.MESH,
+        )
+
+    def hidden_copy(p):
+        return pltpu.make_async_remote_copy(
+            src_ref=hid.at[0, p],
+            dst_ref=hid.at[1, p],
+            send_sem=s2.at[p],
+            recv_sem=r2.at[p],
+            device_id=partner,
+            device_id_type=pl.DeviceIdType.MESH,
+        )
+
+    def down(t, e, side, p):
+        load(t).wait()
+        w = wbuf.at[t % SLOTS]
+
+        @pl.loop(0, cols // D_STEP)
+        def _(k):
+            at = pl.ds(pl.multiple_of(k * D_STEP, D_STEP), D_STEP)
+            acc = jnp.dot(hid[side, p], w[:, at], preferred_element_type=jnp.float32)
+            out_ref[e, :, at] = acc.astype(jnp.bfloat16)
+
+        refill(t)
+
+    t = 0
+    for p in range(pairs):
+        for g in range(2):
+            gate_part(t, theirs[p], sent.at[p, g])
+            reduce_copy(p, g).start()
+            t += 1
+    for p in range(pairs):
+        for g in range(2):
+            gate_part(t, mine[p], kept.at[p, g])
+            t += 1
+    for p in range(pairs):
+        for g in range(2):
+            reduce_copy(p, g).wait_recv()
+
+        @pl.loop(0, rows // 16)
+        def _(k):
+            at = pl.ds(pl.multiple_of(k * 16, 16), 16)
+            gate = kept[p, 0, at, :].astype(jnp.float32) + got[p, 0, at, :].astype(jnp.float32)
+            up = kept[p, 1, at, :].astype(jnp.float32) + got[p, 1, at, :].astype(jnp.float32)
+            hid[0, p, at, :] = (gate / (1.0 + jnp.exp(-gate)) * up).astype(jnp.bfloat16)
+
+        hidden_copy(p).start()
+        down(t, mine[p], 0, p)
+        t += 1
+    for p in range(pairs):
+        hidden_copy(p).wait_recv()
+        down(t, theirs[p], 1, p)
+        t += 1
+    for p in range(pairs):
+        for g in range(2):
+            reduce_copy(p, g).wait_send()
+        hidden_copy(p).wait_send()
+
+
+def expert_rows(picked, gate_up, down_t):
+    owned, rows, cols = picked.shape
+    hidden = gate_up.shape[3]
+    pairs = owned // 2
+    wg = gate_up.transpose(0, 2, 3, 1).reshape(owned * 2, hidden, cols)
+    wd = down_t.transpose(0, 2, 1)
+    vmem = pl.BlockSpec(memory_space=pltpu.VMEM)
+    hbm = pl.BlockSpec(memory_space=pl.ANY)
+    half = (pairs, 2, rows, hidden)
+    return pl.pallas_call(
+        expert_kernel,
+        out_shape=jax.ShapeDtypeStruct((owned, rows, cols), jnp.bfloat16),
+        in_specs=[vmem, hbm, hbm],
+        out_specs=vmem,
+        scratch_shapes=[
+            pltpu.VMEM((SLOTS, hidden, cols), jnp.bfloat16),
+            pltpu.VMEM(half, jnp.bfloat16),
+            pltpu.VMEM(half, jnp.bfloat16),
+            pltpu.VMEM(half, jnp.bfloat16),
+            pltpu.VMEM((2, pairs, rows, hidden), jnp.bfloat16),
+            pltpu.SemaphoreType.DMA((SLOTS,)),
+            pltpu.SemaphoreType.DMA((pairs, 2)),
+            pltpu.SemaphoreType.DMA((pairs, 2)),
+            pltpu.SemaphoreType.DMA((pairs,)),
+            pltpu.SemaphoreType.DMA((pairs,)),
+        ],
+        compiler_params=pltpu.CompilerParams(
+            collective_id=0, has_side_effects=True, vmem_limit_bytes=56 << 20
+        ),
+        cost_estimate=pl.CostEstimate(
+            flops=6 * owned * rows * cols * hidden,
+            bytes_accessed=6 * owned * cols * hidden,
+            transcendentals=owned * rows * hidden,
+        ),
+    )(picked, wg, wd)
+
+
 def per_device(queries, keys, values, lengths, expert_ids, gate_share, gate_up, down_t):
     n_seq = lax.axis_size("seq")
     n_exp = lax.axis_size("exp")
@@ -121,10 +276,15 @@
     rank = jnp.cumsum(count, axis=2) - count
     block = jnp.arange(n_seq, dtype=jnp.int32)[None, :, None]
     key = jnp.where(match, block * CAP + rank, -1)
-    rows = n_seq * CAP
-    part = rows // n_rep
+    paired = n_rep == 2 and owned % 2 == 0 and cols % D_STEP == 0
+    slots = n_seq * CAP
+    rows = -(-slots // 16) * 16 if paired else slots
+    part = slots // n_rep
     at = jnp.arange(rows, dtype=jnp.int32)
-    slot = (r ^ (at // part)) * part + at % part
+    if paired:
+        slot = jnp.where(at < slots, at, -2)
+    else:
+        slot = (r ^ (at // part)) * part + at % part
     pick = (key.reshape(owned, 1, n_seq * tok) == slot[None, :, None]).astype(jnp.bfloat16)
 
     def turned(x):
@@ -140,20 +300,27 @@
     own = attend(queries, keys, values, lengths, kv_here, split)
     tokens = gather_tokens(own, tok, cols, split)
 
-    outs = []
-    for i in range(owned):
-        picked = jnp.dot(pick[i], tokens, preferred_element_type=jnp.float32).astype(jnp.bfloat16)
-        both = jnp.einsum("rd,dgf->grf", picked, gate_up[i], preferred_element_type=jnp.float32)
-        both = both.astype(jnp.bfloat16)
-        total = both[:, :part].astype(jnp.float32)
-        for d in range(1, n_rep):
-            got = swap(both[:, d * part : (d + 1) * part], "rep", d)
-            total = total + got.astype(jnp.float32)
-        hidden = (jax.nn.silu(total[0]) * total[1]).astype(jnp.bfloat16)
-        hidden = jnp.concatenate([hidden] + [swap(hidden, "rep", d) for d in range(1, n_rep)], 0)
-        down = jnp.einsum("rf,df->rd", hidden, down_t[i], preferred_element_type=jnp.float32)
-        outs.append(down.astype(jnp.bfloat16))
-    outs = jnp.concatenate(outs, 0)
+    if paired:
+        picked = jnp.dot(
+            pick.reshape(owned * rows, n_seq * tok), tokens, preferred_element_type=jnp.float32
+        ).astype(jnp.bfloat16)
+        outs = expert_rows(picked.reshape(owned, rows, cols), gate_up, down_t)
+        outs = outs.reshape(owned * rows, cols)
+    else:
+        outs = []
+        for i in range(owned):
+            picked = jnp.dot(pick[i], tokens, preferred_element_type=jnp.float32).astype(jnp.bfloat16)
+            both = jnp.einsum("rd,dgf->grf", picked, gate_up[i], preferred_element_type=jnp.float32)
+            both = both.astype(jnp.bfloat16)
+            total = both[:, :part].astype(jnp.float32)
+            for d in range(1, n_rep):
+                got = swap(both[:, d * part : (d + 1) * part], "rep", d)
+                total = total + got.astype(jnp.float32)
+            hidden = (jax.nn.silu(total[0]) * total[1]).astype(jnp.bfloat16)
+            hidden = jnp.concatenate([hidden] + [swap(hidden, "rep", d) for d in range(1, n_rep)], 0)
+            down = jnp.einsum("rf,df->rd", hidden, down_t[i], preferred_element_type=jnp.float32)
+            outs.append(down.astype(jnp.bfloat16))
+        outs = jnp.concatenate(outs, 0)
 
     results = []
     wide = cols // TAIL_PIECES

time: 186 us -> 156 us (0.84)
  Pallas kernels: 0 us -> 67.5 us
  matrix products: 66.1 us -> 8.9 us
  waiting for transfers between devices: 64.1 us -> 39.9 us
  starting transfers between devices: 34.7 us -> 28.2 us
  local copies, waits for them, and re-layouts: 10.2 us -> 4.46 us
  other arithmetic: 9.79 us -> 6.65 us
    pallas_call x0 -> x1, Pallas kernels: none -> 67.5 us  [expert_rows(): pl.pallas_call(expert_kernel, out_shape=jax.ShapeDtypeStruct((owned, rows...]
    dot_general x8 -> x1, matrix products: 62.6 us -> 3.75 us  [per_device(): jnp.dot(pick.reshape(owned * rows, n_seq * tok), tokens, preferred_elemen...]
    ppermute x31 -> x23, waiting for transfers between devices: 64.1 us -> 39.9 us  [swap(): return lax.ppermute(x, axis, [(i, i ^ distance) for i in range(n)])]
    ppermute x31 -> x23, starting transfers between devices: 27.9 us -> 21.4 us  [swap(): return lax.ppermute(x, axis, [(i, i ^ distance) for i in range(n)])]
    slice x4 -> x0, local copies, waits for them, and re-layouts: 5.2 us -> none  [per_device(): got = swap(both[:, d * part:(d + 1) * part], 'rep', d)]
  transfers between devices with their start and end apart: 33 -> 25, of which waited for: 18 -> 13; matrix products, arithmetic and copies ran while one was open for 22% -> 6% of each run, Pallas kernels for 0% -> 0%
where the time goes in v2:
time: 156 us
  Pallas kernels  67.5 us (43%)
  waiting for transfers between devices  39.9 us (26%)
  starting transfers between devices  28.2 us (18%)
  matrix products  8.9 us (6%)
  other arithmetic  6.65 us (4%)
  local copies, waits for them, and re-layouts  4.46 us (3%)
    pallas_call x1, Pallas kernels, expert_rows(): pl.pallas_call(expert_kernel, out_shape=jax.ShapeDtypeStruct((owned, rows...  67.5 us
    ppermute x23, waiting for transfers between devices, swap(): return lax.ppermute(x, axis, [(i, i ^ distance) for i in range(n)])  39.9 us
    ppermute x23, starting transfers between devices, swap(): return lax.ppermute(x, axis, [(i, i ^ distance) for i in range(n)])  21.4 us
    ppermute x2, starting transfers between devices, shift(): lax.ppermute(x, axis, [(i, i + distance) for i in range(n - distance)])  6.79 us
    dot_general x2, matrix products, per_device(): jnp.dot(spread, outs[:, c * wide:(c + 1) * wide], preferred_element_type=...  4.47 us
    dot_general x1, matrix products, per_device(): jnp.dot(pick.reshape(owned * rows, n_seq * tok), tokens, preferred_elemen...  3.75 us
  transfers between devices with their start and end apart: 25, of which 13 were waited for; matrix products, arithmetic and copies ran while one was open for 6% of the time, Pallas kernels for 0%

profile of v2, /device:TPU:0, one launch (start us, length us, event | category | flops | bytes accessed | tf_op | source)
XLA Modules:
  0.0 156.1 jit_solution(10194461993137520638)
XLA Ops:
  0.0 0.9 constant_dynamic-slice_fusion.1
  0.9 2.4 %collective-permute-start.3 = (bf16[128,256]{1,0:T(8,128)(2,1)S(1)}, bf16[128,256]{1,0:T(8,128)(2,1)S(1)}, u32[]{:S(2)}, u32[]{:S(2)}) collective-permute-start(bf16[128,256]{1,0:T(8,128)(2,1)S(1)} %pad_maximum_fusion.9), channel_id=1, source_target_pairs={{0,8},{8,16},{16,24},{1,9},{9,17},{17,25},{2,10},{10,18},{18,26},{... | collective-permute-start | bytes 196616 | tf_op jit(solution)/shard_map/ppermute | solution.py:28
  3.3 4.4 %collective-permute-start.2 = (bf16[128,256]{1,0:T(8,128)(2,1)S(1)}, bf16[128,256]{1,0:T(8,128)(2,1)S(1)}, u32[]{:S(2)}, u32[]{:S(2)}) collective-permute-start(bf16[128,256]{1,0:T(8,128)(2,1)S(1)} %pad_maximum_fusion.9), channel_id=1, source_target_pairs={{0,16},{8,24},{1,17},{9,25},{2,18},{10,26},{3,19},{11,27},{4,20},{... | collective-permute-start | bytes 196616 | tf_op jit(solution)/shard_map/ppermute | solution.py:28
  7.7 0.7 convert_bitcast_fusion
  8.4 0.7 fusion.35
  9.3 0.8 reduce-window.8
  10.3 0.2 and_and_fusion
  10.5 2.2 %collective-permute-done = f32[1,8,128]{2,1,0:T(8,128)S(1)} collective-permute-done((f32[1,8,128]{2,1,0:T(8,128)S(1)}, f32[1,8,128]{2,1,0:T(8,128)S(1)}, u32[]{:S(2)}, u32[]{:S(2)}) %collective-permute-start) | collective-permute-done | bytes 4128 | tf_op jit(solution)/shard_map/ppermute | solution.py:23
  13.2 0.7 collective-permute-done.1
  14.1 1.2 reduce_window_sum.22
  15.4 0.2 broadcast_compare_fusion
  15.7 0.6 gather_fusion
  16.5 0.3 fusion.37
  16.8 0.2 fusion.7
  17.0 0.4 convolution_convert_fusion.3
  17.7 1.6 %collective-permute-start.6 = (bf16[128,768]{1,0:T(8,128)(2,1)S(1)}, bf16[128,768]{1,0:T(8,128)(2,1)S(1)}, u32[]{:S(2)}, u32[]{:S(2)}) collective-permute-start(bf16[128,768]{1,0:T(8,128)(2,1)S(1)} %copy.80), channel_id=1, source_target_pairs={{0,2},{2,0},{4,6},{6,4},{1,3},{3,1},{5,7},{7,5},{8,10},{10,8},{12,... | collective-permute-start | bytes 589832 | tf_op jit(solution)/shard_map/ppermute | solution.py:23
  19.4 2.6 %collective-permute-start.9 = (bf16[128,768]{1,0:T(8,128)(2,1)S(1)}, bf16[128,768]{1,0:T(8,128)(2,1)S(1)}, u32[]{:S(2)}, u32[]{:S(2)}) collective-permute-start(bf16[128,768]{1,0:T(8,128)(2,1)S(1)} %copy.80), channel_id=1, source_target_pairs={{0,4},{2,6},{4,0},{6,2},{1,5},{3,7},{5,1},{7,3},{8,12},{10,14},{12... | collective-permute-start | bytes 589832 | tf_op jit(solution)/shard_map/ppermute | solution.py:23
  22.2 0.6 gather_fusion.1
  22.9 0.2 collective-permute-start.12
  23.2 1.3 collective-permute-done.4
  24.7 3.7 %collective-permute-done.6 = bf16[128,768]{1,0:T(8,128)(2,1)S(1)} collective-permute-done((bf16[128,768]{1,0:T(8,128)(2,1)S(1)}, bf16[128,768]{1,0:T(8,128)(2,1)S(1)}, u32[]{:S(2)}, u32[]{:S(2)}) %collective-permute-start.6) | collective-permute-done | bytes 196640 | tf_op jit(solution)/shard_map/ppermute | solution.py:23
  28.4 1.6 %collective-permute-start.7 = (bf16[1,1,128,768]{3,2,1,0:T(8,128)(2,1)S(1)}, bf16[1,1,128,768]{3,2,1,0:T(8,128)(2,1)S(1)}, u32[]{:S(2)}, u32[]{:S(2)}) collective-permute-start(bf16[1,1,128,768]{3,2,1,0:T(8,128)(2,1)S(1)} %bitcast.223), channel_id=1, source_target_pairs={{0,16},{8,24},{16,0},{24,8},{1,17},{9,25},{17,1},{25,9},{2,18},{10... | collective-permute-start | bytes 589832 | tf_op jit(solution)/shard_map/ppermute | solution.py:23
  30.0 6.5 %collective-permute-done.9 = bf16[128,768]{1,0:T(8,128)(2,1)S(1)} collective-permute-done((bf16[128,768]{1,0:T(8,128)(2,1)S(1)}, bf16[128,768]{1,0:T(8,128)(2,1)S(1)}, u32[]{:S(2)}, u32[]{:S(2)}) %collective-permute-start.9) | collective-permute-done | bytes 196640 | tf_op jit(solution)/shard_map/ppermute | solution.py:23
  36.5 2.0 %collective-permute-start.10 = (bf16[1,1,128,768]{3,2,1,0:T(8,128)(2,1)S(1)}, bf16[1,1,128,768]{3,2,1,0:T(8,128)(2,1)S(1)}, u32[]{:S(2)}, u32[]{:S(2)}) collective-permute-start(bf16[1,1,128,768]{3,2,1,0:T(8,128)(2,1)S(1)} %bitcast.221), channel_id=1, source_target_pairs={{0,16},{8,24},{16,0},{24,8},{1,17},{9,25},{17,1},{25,9},{2,18},{10... | collective-permute-start | bytes 589832 | tf_op jit(solution)/shard_map/ppermute | solution.py:23
  38.5 0.2 fusion.6
  39.0 3.2 %collective-permute-done.10 = bf16[1,1,128,768]{3,2,1,0:T(8,128)(2,1)S(1)} collective-permute-done((bf16[1,1,128,768]{3,2,1,0:T(8,128)(2,1)S(1)}, bf16[1,1,128,768]{3,2,1,0:T(8,128)(2,1)S(1)}, u32[]{:S(2)}, u32[]{:S(2)}) %collective-permute-start.10) | collective-permute-done | bytes 196640 | tf_op jit(solution)/shard_map/ppermute | solution.py:23
  42.3 2.1 %collective-permute-done.13 = bf16[1,1,128,768]{3,2,1,0:T(8,128)(2,1)S(1)} collective-permute-done((bf16[1,1,128,768]{3,2,1,0:T(8,128)(2,1)S(1)}, bf16[1,1,128,768]{3,2,1,0:T(8,128)(2,1)S(1)}, u32[]{:S(2)}, u32[]{:S(2)}) %collective-permute-start.13) | collective-permute-done | bytes 196640 | tf_op jit(solution)/shard_map/ppermute | solution.py:23
  44.7 0.4 broadcast_in_dim.110
  45.4 0.9 collective-permute-done.14
  46.7 3.7 %convolution_convert_fusion = bf16[576,3072]{1,0:T(8,128)(2,1)} fusion(pred[576,512]{1,0:T(8,128)(4,1)S(1)} %bitcast.220, bf16[512,3072]{1,0:T(8,128)(2,1)S(1)} %bitcast.207), kind=kOutput, calls=%fused_computation.2 | convolution fusion | flops 1813708800 | bytes 6979584 | tf_op jit(solution)/shard_map/dot_general | solution.py:304
  50.5 67.5 %shard_map.82 = bf16[4,144,3072]{2,1,0:T(8,128)(2,1)} custom-call(bf16[4,144,3072]{2,1,0:T(8,128)(2,1)} %bitcast.202, bf16[8,1344,3072]{2,1,0:T(8,128)(2,1)} %bitcast.198, bf16[4,1344,3072]{2,1,0:T(8,128)(2,1)} %bitcast.199), custom_call_target="tpu_custom_call" | custom-call | flops 14269022208 | bytes 99090432 | tf_op jit(solution)/shard_map/pallas_call | solution.py:228
  117.9 3.0 %convolution_convert_fusion.1 = bf16[512,1536]{1,0:T(8,128)(2,1)S(1)} fusion(bf16[512,576]{0,1:T(8,128)(2,1)S(1)} %fusion.6, bf16[576,3072]{1,0:T(8,128)(2,1)} %bitcast.200), kind=kOutput, calls=%fused_computation.3 | convolution fusion | flops 906756096 | bytes 3932160 | tf_op jit(solution)/shard_map/dot_general | solution.py:328
  121.1 1.4 convolution_convert_fusion.2
  122.6 0.6 collective-permute-start.15
  123.2 0.2 collective-permute-done.20
  123.4 0.2 fusion.9
  123.6 1.9 %collective-permute-start.21 = (bf16[1,128,1536]{2,1,0:T(8,128)(2,1)S(1)}, bf16[1,128,1536]{2,1,0:T(8,128)(2,1)S(1)}, u32[]{:S(2)}, u32[]{:S(2)}) collective-permute-start(bf16[1,128,1536]{2,1,0:T(8,128)(2,1)S(1)} %slice_bitcast_fusion.4), channel_id=1, source_target_pairs={{0,16},{8,24},{16,0},{24,8},{1,17},{9,25},{17,1},{25,9},{2,18},{10... | collective-permute-start | bytes 1179656 | tf_op jit(solution)/shard_map/ppermute | solution.py:23
  125.5 0.2 fusion.8
  125.8 1.5 collective-permute-start.16
  127.3 8.4 %collective-permute-done.21 = bf16[1,128,1536]{2,1,0:T(8,128)(2,1)S(1)} collective-permute-done((bf16[1,128,1536]{2,1,0:T(8,128)(2,1)S(1)}, bf16[1,128,1536]{2,1,0:T(8,128)(2,1)S(1)}, u32[]{:S(2)}, u32[]{:S(2)}) %collective-permute-start.21) | collective-permute-done | bytes 393248 | tf_op jit(solution)/shard_map/ppermute | solution.py:23
  135.8 3.6 %collective-permute-start.24 = (bf16[32,1536]{1,0:T(8,128)(2,1)S(1)}, bf16[32,1536]{1,0:T(8,128)(2,1)S(1)}, u32[]{:S(2)}, u32[]{:S(2)}) collective-permute-start(bf16[32,1536]{1,0:T(8,128)(2,1)S(1)} %get-tuple-element.9), channel_id=1, source_target_pairs={{0,6},{2,4},{4,2},{6,0},{1,7},{3,5},{5,3},{7,1},{8,14},{10,12},{12... | collective-permute-start | bytes 294920 | tf_op jit(solution)/shard_map/ppermute | solution.py:23
  139.4 0.8 collective-permute-start.22
  140.2 3.2 %collective-permute-done.16 = bf16[1,128,1536]{2,1,0:T(8,128)(2,1)S(1)} collective-permute-done((bf16[1,128,1536]{2,1,0:T(8,128)(2,1)S(1)}, bf16[1,128,1536]{2,1,0:T(8,128)(2,1)S(1)}, u32[]{:S(2)}, u32[]{:S(2)}) %collective-permute-start.16) | collective-permute-done | bytes 393248 | tf_op jit(solution)/shard_map/ppermute | solution.py:23
  143.5 3.5 %collective-permute-start.19 = (bf16[32,1536]{1,0:T(8,128)(2,1)S(1)}, bf16[32,1536]{1,0:T(8,128)(2,1)S(1)}, u32[]{:S(2)}, u32[]{:S(2)}) collective-permute-start(bf16[32,1536]{1,0:T(8,128)(2,1)S(1)} %get-tuple-element.6), channel_id=1, source_target_pairs={{0,6},{2,4},{4,2},{6,0},{1,7},{3,5},{5,3},{7,1},{8,14},{10,12},{12... | collective-permute-start | bytes 294920 | tf_op jit(solution)/shard_map/ppermute | solution.py:23
  147.0 1.0 collective-permute-start.17
  148.0 2.8 %collective-permute-done.19 = bf16[32,1536]{1,0:T(8,128)(2,1)S(1)} collective-permute-done((bf16[32,1536]{1,0:T(8,128)(2,1)S(1)}, bf16[32,1536]{1,0:T(8,128)(2,1)S(1)}, u32[]{:S(2)}, u32[]{:S(2)}) %collective-permute-start.19) | collective-permute-done | bytes 98336 | tf_op jit(solution)/shard_map/ppermute | solution.py:23
  150.8 4.5 %collective-permute-done.18 = bf16[32,1536]{1,0:T(8,128)(2,1)S(1)} collective-permute-done((bf16[32,1536]{1,0:T(8,128)(2,1)S(1)}, bf16[32,1536]{1,0:T(8,128)(2,1)S(1)}, u32[]{:S(2)}, u32[]{:S(2)}) %collective-permute-start.18) | collective-permute-done | bytes 98336 | tf_op jit(solution)/shard_map/ppermute | solution.py:23
  155.4 0.7 pad_maximum_fusion.8
  (92 shorter events, 4.0 us)
Async XLA Ops:
  0.0 10.3 %copy-start = (bf16[128,6144]{1,0:T(8,128)(2,1)S(1)}, bf16[128,6144]{1,0:T(8,128)(2,1)}, u32[]{:S(2)}) copy-start(bf16[128,6144]{1,0:T(8,128)(2,1)} %param.8) | copy-start | bytes 4718596
  0.9 15.5 %collective-permute-start.3 = (bf16[128,256]{1,0:T(8,128)(2,1)S(1)}, bf16[128,256]{1,0:T(8,128)(2,1)S(1)}, u32[]{:S(2)}, u32[]{:S(2)}) collective-permute-start(bf16[128,256]{1,0:T(8,128)(2,1)S(1)} %pad_maximum_fusion.9), channel_id=1, source_target_pairs={{0,8},{8,16},{16,24},{1,9},{9,17},{17,25},{2,10},{10,18},{18,26},{... | collective-permute-start | bytes 196616 | tf_op jit(solution)/shard_map/ppermute | solution.py:28
  3.3 13.2 %collective-permute-start.2 = (bf16[128,256]{1,0:T(8,128)(2,1)S(1)}, bf16[128,256]{1,0:T(8,128)(2,1)S(1)}, u32[]{:S(2)}, u32[]{:S(2)}) collective-permute-start(bf16[128,256]{1,0:T(8,128)(2,1)S(1)} %pad_maximum_fusion.9), channel_id=1, source_target_pairs={{0,16},{8,24},{1,17},{9,25},{2,18},{10,26},{3,19},{11,27},{4,20},{... | collective-permute-start | bytes 196616 | tf_op jit(solution)/shard_map/ppermute | solution.py:28
  9.1 3.6 %collective-permute-start = (f32[1,8,128]{2,1,0:T(8,128)S(1)}, f32[1,8,128]{2,1,0:T(8,128)S(1)}, u32[]{:S(2)}, u32[]{:S(2)}) collective-permute-start(f32[1,8,128]{2,1,0:T(8,128)S(1)} %get-tuple-element.24), channel_id=1, source_target_pairs={{0,16},{8,24},{16,0},{24,8},{1,17},{9,25},{17,1},{25,9},{2,18},{10... | collective-permute-start | bytes 12296 | tf_op jit(solution)/shard_map/ppermute | solution.py:23
  12.7 1.2 collective-permute-start.1
  17.5 7.0 %collective-permute-start.4 = (bf16[1,1,128,768]{3,2,1,0:T(8,128)(2,1)S(1)}, bf16[1,1,128,768]{3,2,1,0:T(8,128)(2,1)S(1)}, u32[]{:S(2)}, u32[]{:S(2)}) collective-permute-start(bf16[1,1,128,768]{3,2,1,0:T(8,128)(2,1)S(1)} %copy.77), channel_id=1, source_target_pairs={{0,16},{8,24},{16,0},{24,8},{1,17},{9,25},{17,1},{25,9},{2,18},{10... | collective-permute-start | bytes 589832 | tf_op jit(solution)/shard_map/ppermute | solution.py:23
  17.7 10.7 %collective-permute-start.6 = (bf16[128,768]{1,0:T(8,128)(2,1)S(1)}, bf16[128,768]{1,0:T(8,128)(2,1)S(1)}, u32[]{:S(2)}, u32[]{:S(2)}) collective-permute-start(bf16[128,768]{1,0:T(8,128)(2,1)S(1)} %copy.80), channel_id=1, source_target_pairs={{0,2},{2,0},{4,6},{6,4},{1,3},{3,1},{5,7},{7,5},{8,10},{10,8},{12,... | collective-permute-start | bytes 589832 | tf_op jit(solution)/shard_map/ppermute | solution.py:23
  19.4 17.1 %collective-permute-start.9 = (bf16[128,768]{1,0:T(8,128)(2,1)S(1)}, bf16[128,768]{1,0:T(8,128)(2,1)S(1)}, u32[]{:S(2)}, u32[]{:S(2)}) collective-permute-start(bf16[128,768]{1,0:T(8,128)(2,1)S(1)} %copy.80), channel_id=1, source_target_pairs={{0,4},{2,6},{4,0},{6,2},{1,5},{3,7},{5,1},{7,3},{8,12},{10,14},{12... | collective-permute-start | bytes 589832 | tf_op jit(solution)/shard_map/ppermute | solution.py:23
  22.9 15.9 %collective-permute-start.12 = (bf16[128,768]{1,0:T(8,128)(2,1)S(1)}, bf16[128,768]{1,0:T(8,128)(2,1)S(1)}, u32[]{:S(2)}, u32[]{:S(2)}) collective-permute-start(bf16[128,768]{1,0:T(8,128)(2,1)S(1)} %copy.80), channel_id=1, source_target_pairs={{0,6},{2,4},{4,2},{6,0},{1,7},{3,5},{5,3},{7,1},{8,14},{10,12},{12... | collective-permute-start | bytes 589832 | tf_op jit(solution)/shard_map/ppermute | solution.py:23
  24.6 20.0 %collective-permute-start.5 = (bf16[2,1,128,768]{3,2,0,1:T(8,128)(2,1)S(1)}, bf16[2,1,128,768]{3,2,0,1:T(8,128)(2,1)S(1)}, u32[]{:S(2)}, u32[]{:S(2)}) collective-permute-start(bf16[2,1,128,768]{3,2,0,1:T(8,128)(2,1)S(1)} %get-tuple-element.18), channel_id=1, source_target_pairs={{0,8},{8,0},{16,24},{24,16},{1,9},{9,1},{17,25},{25,17},{2,10},{10... | collective-permute-start | bytes 1179656 | tf_op jit(solution)/shard_map/ppermute | solution.py:23
  28.4 10.4 %collective-permute-start.7 = (bf16[1,1,128,768]{3,2,1,0:T(8,128)(2,1)S(1)}, bf16[1,1,128,768]{3,2,1,0:T(8,128)(2,1)S(1)}, u32[]{:S(2)}, u32[]{:S(2)}) collective-permute-start(bf16[1,1,128,768]{3,2,1,0:T(8,128)(2,1)S(1)} %bitcast.223), channel_id=1, source_target_pairs={{0,16},{8,24},{16,0},{24,8},{1,17},{9,25},{17,1},{25,9},{2,18},{10... | collective-permute-start | bytes 589832 | tf_op jit(solution)/shard_map/ppermute | solution.py:23
  36.5 5.7 %collective-permute-start.10 = (bf16[1,1,128,768]{3,2,1,0:T(8,128)(2,1)S(1)}, bf16[1,1,128,768]{3,2,1,0:T(8,128)(2,1)S(1)}, u32[]{:S(2)}, u32[]{:S(2)}) collective-permute-start(bf16[1,1,128,768]{3,2,1,0:T(8,128)(2,1)S(1)} %bitcast.221), channel_id=1, source_target_pairs={{0,16},{8,24},{16,0},{24,8},{1,17},{9,25},{17,1},{25,9},{2,18},{10... | collective-permute-start | bytes 589832 | tf_op jit(solution)/shard_map/ppermute | solution.py:23
  38.7 5.7 %collective-permute-start.13 = (bf16[1,1,128,768]{3,2,1,0:T(8,128)(2,1)S(1)}, bf16[1,1,128,768]{3,2,1,0:T(8,128)(2,1)S(1)}, u32[]{:S(2)}, u32[]{:S(2)}) collective-permute-start(bf16[1,1,128,768]{3,2,1,0:T(8,128)(2,1)S(1)} %bitcast.225), channel_id=1, source_target_pairs={{0,16},{8,24},{16,0},{24,8},{1,17},{9,25},{17,1},{25,9},{2,18},{10... | collective-permute-start | bytes 589832 | tf_op jit(solution)/shard_map/ppermute | solution.py:23
  38.9 6.3 %collective-permute-start.8 = (bf16[2,1,128,768]{3,2,0,1:T(8,128)(2,1)S(1)}, bf16[2,1,128,768]{3,2,0,1:T(8,128)(2,1)S(1)}, u32[]{:S(2)}, u32[]{:S(2)}) collective-permute-start(bf16[2,1,128,768]{3,2,0,1:T(8,128)(2,1)S(1)} %get-tuple-element.16), channel_id=1, source_target_pairs={{0,8},{8,0},{16,24},{24,16},{1,9},{9,1},{17,25},{25,17},{2,10},{10... | collective-permute-start | bytes 1179656 | tf_op jit(solution)/shard_map/ppermute | solution.py:23
  42.2 3.0 %collective-permute-start.11 = (bf16[2,1,128,768]{3,2,0,1:T(8,128)(2,1)S(1)}, bf16[2,1,128,768]{3,2,0,1:T(8,128)(2,1)S(1)}, u32[]{:S(2)}, u32[]{:S(2)}) collective-permute-start(bf16[2,1,128,768]{3,2,0,1:T(8,128)(2,1)S(1)} %get-tuple-element.14), channel_id=1, source_target_pairs={{0,8},{8,0},{16,24},{24,16},{1,9},{9,1},{17,25},{25,17},{2,10},{10... | collective-permute-start | bytes 1179656 | tf_op jit(solution)/shard_map/ppermute | solution.py:23
  44.5 1.8 %collective-permute-start.14 = (bf16[2,1,128,768]{3,2,0,1:T(8,128)(2,1)S(1)}, bf16[2,1,128,768]{3,2,0,1:T(8,128)(2,1)S(1)}, u32[]{:S(2)}, u32[]{:S(2)}) collective-permute-start(bf16[2,1,128,768]{3,2,0,1:T(8,128)(2,1)S(1)} %get-tuple-element.12), channel_id=1, source_target_pairs={{0,8},{8,0},{16,24},{24,16},{1,9},{9,1},{17,25},{25,17},{2,10},{10... | collective-permute-start | bytes 1179656 | tf_op jit(solution)/shard_map/ppermute | solution.py:23
  117.9 3.2 %copy-start.2 = (bf16[4,144,3072]{2,1,0:T(8,128)(2,1)S(1)}, bf16[4,144,3072]{2,1,0:T(8,128)(2,1)}, u32[]{:S(2)}) copy-start(bf16[4,144,3072]{2,1,0:T(8,128)(2,1)} %shard_map.82) | copy-start | bytes 10616836
  121.1 2.4 %collective-permute-start.20 = (bf16[2,128,1536]{2,1,0:T(8,128)(2,1)S(1)}, bf16[2,128,1536]{2,1,0:T(8,128)(2,1)S(1)}, u32[]{:S(2)}, u32[]{:S(2)}) collective-permute-start(bf16[2,128,1536]{2,1,0:T(8,128)(2,1)S(1)} %slice_bitcast_fusion), channel_id=1, source_target_pairs={{0,8},{8,0},{16,24},{24,16},{1,9},{9,1},{17,25},{25,17},{2,10},{10... | collective-permute-start | bytes 2359304 | tf_op jit(solution)/shard_map/ppermute | solution.py:23
  122.6 2.9 %collective-permute-start.15 = (bf16[2,128,1536]{2,1,0:T(8,128)(2,1)S(1)}, bf16[2,128,1536]{2,1,0:T(8,128)(2,1)S(1)}, u32[]{:S(2)}, u32[]{:S(2)}) collective-permute-start(bf16[2,128,1536]{2,1,0:T(8,128)(2,1)S(1)} %slice_bitcast_fusion.2), channel_id=1, source_target_pairs={{0,8},{8,0},{16,24},{24,16},{1,9},{9,1},{17,25},{25,17},{2,10},{10... | collective-permute-start | bytes 2359304 | tf_op jit(solution)/shard_map/ppermute | solution.py:23
  123.6 12.0 %collective-permute-start.21 = (bf16[1,128,1536]{2,1,0:T(8,128)(2,1)S(1)}, bf16[1,128,1536]{2,1,0:T(8,128)(2,1)S(1)}, u32[]{:S(2)}, u32[]{:S(2)}) collective-permute-start(bf16[1,128,1536]{2,1,0:T(8,128)(2,1)S(1)} %slice_bitcast_fusion.4), channel_id=1, source_target_pairs={{0,16},{8,24},{16,0},{24,8},{1,17},{9,25},{17,1},{25,9},{2,18},{10... | collective-permute-start | bytes 1179656 | tf_op jit(solution)/shard_map/ppermute | solution.py:23
  125.8 17.6 %collective-permute-start.16 = (bf16[1,128,1536]{2,1,0:T(8,128)(2,1)S(1)}, bf16[1,128,1536]{2,1,0:T(8,128)(2,1)S(1)}, u32[]{:S(2)}, u32[]{:S(2)}) collective-permute-start(bf16[1,128,1536]{2,1,0:T(8,128)(2,1)S(1)} %slice_bitcast_fusion.6), channel_id=1, source_target_pairs={{0,16},{8,24},{16,0},{24,8},{1,17},{9,25},{17,1},{25,9},{2,18},{10... | collective-permute-start | bytes 1179656 | tf_op jit(solution)/shard_map/ppermute | solution.py:23
  135.8 11.2 %collective-permute-start.24 = (bf16[32,1536]{1,0:T(8,128)(2,1)S(1)}, bf16[32,1536]{1,0:T(8,128)(2,1)S(1)}, u32[]{:S(2)}, u32[]{:S(2)}) collective-permute-start(bf16[32,1536]{1,0:T(8,128)(2,1)S(1)} %get-tuple-element.9), channel_id=1, source_target_pairs={{0,6},{2,4},{4,2},{6,0},{1,7},{3,5},{5,3},{7,1},{8,14},{10,12},{12... | collective-permute-start | bytes 294920 | tf_op jit(solution)/shard_map/ppermute | solution.py:23
  139.4 8.6 %collective-permute-start.23 = (bf16[32,1536]{1,0:T(8,128)(2,1)S(1)}, bf16[32,1536]{1,0:T(8,128)(2,1)S(1)}, u32[]{:S(2)}, u32[]{:S(2)}) collective-permute-start(bf16[32,1536]{1,0:T(8,128)(2,1)S(1)} %get-tuple-element.10), channel_id=1, source_target_pairs={{0,4},{2,6},{4,0},{6,2},{1,5},{3,7},{5,1},{7,3},{8,12},{10,14},{12... | collective-permute-start | bytes 294920 | tf_op jit(solution)/shard_map/ppermute | solution.py:23
  139.4 16.7 %copy-start.1 = (bf16[128,6144]{1,0:T(8,128)(2,1)S(1)}, bf16[128,6144]{1,0:T(8,128)(2,1)}, u32[]{:S(2)}) copy-start(bf16[128,6144]{1,0:T(8,128)(2,1)} %param.8) | copy-start | bytes 4718596
  139.4 8.6 %collective-permute-start.22 = (bf16[32,1536]{1,0:T(8,128)(2,1)S(1)}, bf16[32,1536]{1,0:T(8,128)(2,1)S(1)}, u32[]{:S(2)}, u32[]{:S(2)}) collective-permute-start(bf16[32,1536]{1,0:T(8,128)(2,1)S(1)} %get-tuple-element.8), channel_id=1, source_target_pairs={{0,2},{2,0},{4,6},{6,4},{1,3},{3,1},{5,7},{7,5},{8,10},{10,8},{12,... | collective-permute-start | bytes 294920 | tf_op jit(solution)/shard_map/ppermute | solution.py:23
  143.5 7.3 %collective-permute-start.19 = (bf16[32,1536]{1,0:T(8,128)(2,1)S(1)}, bf16[32,1536]{1,0:T(8,128)(2,1)S(1)}, u32[]{:S(2)}, u32[]{:S(2)}) collective-permute-start(bf16[32,1536]{1,0:T(8,128)(2,1)S(1)} %get-tuple-element.6), channel_id=1, source_target_pairs={{0,6},{2,4},{4,2},{6,0},{1,7},{3,5},{5,3},{7,1},{8,14},{10,12},{12... | collective-permute-start | bytes 294920 | tf_op jit(solution)/shard_map/ppermute | solution.py:23
  147.0 8.4 %collective-permute-start.18 = (bf16[32,1536]{1,0:T(8,128)(2,1)S(1)}, bf16[32,1536]{1,0:T(8,128)(2,1)S(1)}, u32[]{:S(2)}, u32[]{:S(2)}) collective-permute-start(bf16[32,1536]{1,0:T(8,128)(2,1)S(1)} %get-tuple-element.7), channel_id=1, source_target_pairs={{0,4},{2,6},{4,0},{6,2},{1,5},{3,7},{5,1},{7,3},{8,12},{10,14},{12... | collective-permute-start | bytes 294920 | tf_op jit(solution)/shard_map/ppermute | solution.py:23
  147.0 8.4 %collective-permute-start.17 = (bf16[32,1536]{1,0:T(8,128)(2,1)S(1)}, bf16[32,1536]{1,0:T(8,128)(2,1)S(1)}, u32[]{:S(2)}, u32[]{:S(2)}) collective-permute-start(bf16[32,1536]{1,0:T(8,128)(2,1)S(1)} %get-tuple-element.5), channel_id=1, source_target_pairs={{0,2},{2,0},{4,6},{6,4},{1,3},{3,1},{5,7},{7,5},{8,10},{10,8},{12,... | collective-permute-start | bytes 294920 | tf_op jit(solution)/shard_map/ppermute | solution.py:23

commit v3 on v2

--- a/solution.py
+++ b/solution.py
@@ -253,6 +253,173 @@
     )(picked, wg, wd)
 
 
+def greet(partners):
+    barrier = pltpu.get_barrier_semaphore()
+    for partner in partners:
+        pl.semaphore_signal(barrier, inc=1, device_id=partner, device_id_type=pl.DeviceIdType.MESH)
+    pl.semaphore_wait(barrier, len(partners))
+
+
+def plane():
+    s = lax.axis_index("seq")
+    e = lax.axis_index("exp")
+    n = lax.axis_size("exp")
+    near = {"seq": s + 1 - 2 * (s % 2)}
+    far = {"seq": (s + 2) % 4}
+    return near, far, [{"exp": (e + d) % n} for d in range(n)]
+
+
+def remote(src, dst, send, recv, device):
+    return pltpu.make_async_remote_copy(
+        src_ref=src,
+        dst_ref=dst,
+        send_sem=send,
+        recv_sem=recv,
+        device_id=device,
+        device_id_type=pl.DeviceIdType.MESH,
+    )
+
+
+def gather_kernel(own, out, zs, zr, ys, yr, cs, cr):
+    e = lax.axis_index("exp")
+    n = lax.axis_size("exp")
+    width = own.shape[1]
+    near, far, line = plane()
+
+    def columns(d):
+        return pl.ds(pl.multiple_of(((e + n - d) % n) * width, 128), width)
+
+    def along_exp(d):
+        return remote(own, out.at[0, :, columns(0)], zs.at[d], zr.at[d], line[d])
+
+    def along_y(d):
+        src = own if d == 0 else out.at[0, :, columns(d)]
+        return remote(src, out.at[2, :, columns(d)], ys.at[d], yr.at[d], far)
+
+    def along_core(d, q):
+        src = own if d == 0 and q == 0 else out.at[2 * q, :, columns(d)]
+        return remote(src, out.at[2 * q + 1, :, columns(d)], cs.at[d, q], cr.at[d, q], near)
+
+    greet([near, far] + line[1:])
+    for d in range(1, n):
+        along_exp(d).start()
+    along_y(0).start()
+    along_core(0, 0).start()
+    out[0, :, columns(0)] = own[...]
+    for d in range(1, n):
+        along_exp(d).wait_recv()
+        along_y(d).start()
+        along_core(d, 0).start()
+        along_y(d - 1).wait_recv()
+        along_core(d - 1, 1).start()
+    along_y(n - 1).wait_recv()
+    along_core(n - 1, 1).start()
+    for d in range(n):
+        for q in range(2):
+            along_core(d, q).wait()
+        along_y(d).wait_send()
+        if d:
+            along_exp(d).wait_send()
+
+
+def gather_plane(own, tok, cols):
+    n = lax.axis_size("exp")
+    vmem = pl.BlockSpec(memory_space=pltpu.VMEM)
+    sems = [pltpu.SemaphoreType.DMA((n,))] * 4 + [pltpu.SemaphoreType.DMA((n, 2))] * 2
+    return pl.pallas_call(
+        gather_kernel,
+        out_shape=jax.ShapeDtypeStruct((4, tok, cols), jnp.bfloat16),
+        in_specs=[vmem],
+        out_specs=vmem,
+        scratch_shapes=sems,
+        compiler_params=pltpu.CompilerParams(
+            collective_id=1, has_side_effects=True, vmem_limit_bytes=16 << 20
+        ),
+    )(own).reshape(4 * tok, cols)
+
+
+def combine_kernel(spread, rows, out, term, cgot, half, ygot, quarter, zgot, cs, cr, ys, yr, zs, zr):
+    n = lax.axis_size("exp")
+    pieces, _, _, tok, width = term.shape
+    mine = tok // n
+    near, far, line = plane()
+
+    def along_core(c):
+        return remote(term.at[c, 1], cgot.at[c], cs.at[c], cr.at[c], near)
+
+    def along_y(c):
+        return remote(half.at[c, 1], ygot.at[c], ys.at[c], yr.at[c], far)
+
+    def along_exp(c, d):
+        src = quarter.at[c, pl.ds(d * mine, mine)]
+        return remote(src, zgot.at[c, d], zs.at[c, d], zr.at[c, d], line[d])
+
+    def wide(x):
+        return x.astype(jnp.float32)
+
+    def first(c):
+        for q in (1, 3, 0, 2):
+            acc = jnp.dot(
+                spread[q * tok : (q + 1) * tok, :],
+                rows[:, c * width : (c + 1) * width],
+                preferred_element_type=jnp.float32,
+            )
+            term[c, q % 2, q // 2] = acc.astype(jnp.bfloat16)
+        along_core(c).start()
+
+    def second(c):
+        along_core(c).wait_recv()
+        half[c, 1] = (wide(term[c, 0, 1]) + wide(cgot[c, 1])).astype(jnp.bfloat16)
+        along_y(c).start()
+        half[c, 0] = (wide(term[c, 0, 0]) + wide(cgot[c, 0])).astype(jnp.bfloat16)
+
+    def third(c):
+        along_y(c).wait_recv()
+        quarter[c] = (wide(half[c, 0]) + wide(ygot[c])).astype(jnp.bfloat16)
+        for d in range(1, n):
+            along_exp(c, d).start()
+
+    greet([near, far] + line[1:])
+    for c in range(pieces + 2):
+        if c < pieces:
+            first(c)
+        if 1 <= c <= pieces:
+            second(c - 1)
+        if c >= 2:
+            third(c - 2)
+    for c in range(pieces):
+        total = wide(quarter[c, :mine])
+        for d in range(1, n):
+            along_exp(c, d).wait_recv()
+            total = total + wide(zgot[c, d])
+        out[:, c * width : (c + 1) * width] = total.astype(jnp.bfloat16)
+    for c in range(pieces):
+        along_core(c).wait_send()
+        along_y(c).wait_send()
+        for d in range(1, n):
+            along_exp(c, d).wait_send()
+
+
+def combine_plane(spread, rows, tok):
+    n = lax.axis_size("exp")
+    cols = rows.shape[1]
+    c, w = 4, cols // 4
+    vmem = pl.BlockSpec(memory_space=pltpu.VMEM)
+    shapes = [(c, 2, 2, tok, w), (c, 2, tok, w), (c, 2, tok, w), (c, tok, w), (c, tok, w)]
+    shapes.append((c, n, tok // n, w))
+    sems = [pltpu.SemaphoreType.DMA((c,))] * 4 + [pltpu.SemaphoreType.DMA((c, n))] * 2
+    return pl.pallas_call(
+        combine_kernel,
+        out_shape=jax.ShapeDtypeStruct((tok // n, cols), jnp.bfloat16),
+        in_specs=[vmem, vmem],
+        out_specs=vmem,
+        scratch_shapes=[pltpu.VMEM(shape, jnp.bfloat16) for shape in shapes] + sems,
+        compiler_params=pltpu.CompilerParams(
+            collective_id=2, has_side_effects=True, vmem_limit_bytes=32 << 20
+        ),
+    )(spread, rows)
+
+
 def per_device(queries, keys, values, lengths, expert_ids, gate_share, gate_up, down_t):
     n_seq = lax.axis_size("seq")
     n_exp = lax.axis_size("exp")
@@ -277,6 +444,7 @@
     block = jnp.arange(n_seq, dtype=jnp.int32)[None, :, None]
     key = jnp.where(match, block * CAP + rank, -1)
     paired = n_rep == 2 and owned % 2 == 0 and cols % D_STEP == 0
+    compact = paired and n_seq == 4 and split == 1 and kv_here == n_exp and cols % 512 == 0
     slots = n_seq * CAP
     rows = -(-slots // 16) * 16 if paired else slots
     part = slots // n_rep
@@ -289,7 +457,8 @@
 
     def turned(x):
         cut = x.reshape(owned, n_seq, n_exp, tok // n_exp)
-        order = e ^ jnp.arange(n_exp, dtype=jnp.int32)
+        order = jnp.arange(n_exp, dtype=jnp.int32)
+        order = (e + order) % n_exp if compact else e ^ order
         return jnp.take(cut, order, axis=2).reshape(owned, n_seq * tok)
 
     key_out, share_out = turned(key), turned(share)
@@ -298,7 +467,10 @@
     ).astype(jnp.bfloat16).reshape(n_seq * tok, owned * rows)
 
     own = attend(queries, keys, values, lengths, kv_here, split)
-    tokens = gather_tokens(own, tok, cols, split)
+    if compact:
+        tokens = gather_plane(own, tok, cols)
+    else:
+        tokens = gather_tokens(own, tok, cols, split)
 
     if paired:
         picked = jnp.dot(
@@ -322,6 +494,9 @@
             outs.append(down.astype(jnp.bfloat16))
         outs = jnp.concatenate(outs, 0)
 
+    if compact:
+        return combine_plane(spread, outs, tok)
+
     results = []
     wide = cols // TAIL_PIECES
     for c in range(TAIL_PIECES):

time: 156 us -> 155 us (level)
  Pallas kernels: 67.5 us -> 129 us
  waiting for transfers between devices: 39.9 us -> 2.94 us
  starting transfers between devices: 28.2 us -> 6.34 us
  matrix products: 8.9 us -> 4.44 us
  local copies, waits for them, and re-layouts: 4.46 us -> 6.74 us
  other arithmetic: 6.65 us -> 4.79 us
    pallas_call x0 -> x2, Pallas kernels: none -> 60.9 us  [the longest x1 32.9 us: combine_plane(): pl.pallas_call(combine_kernel, out_shape=jax.ShapeDtypeStruct((tok // n,...]
    ppermute x23 -> x2, waiting for transfers between devices: 39.9 us -> 2.93 us  [swap(): return lax.ppermute(x, axis, [(i, i ^ distance) for i in range(n)])]
    ppermute x23 -> x2, starting transfers between devices: 21.4 us -> 0.01 us  [swap(): return lax.ppermute(x, axis, [(i, i ^ distance) for i in range(n)])]
    dot_general x2 -> x0, matrix products: 4.47 us -> none  [per_device(): jnp.dot(spread, outs[:, c * wide:(c + 1) * wide], preferred_element_type=...]
    unnamed x7 -> x8, local copies, waits for them, and re-layouts: 0.17 us -> 2.84 us
  transfers between devices with their start and end apart: 25 -> 4, of which waited for: 13 -> 2; matrix products, arithmetic and copies ran while one was open for 6% -> 5% of each run, Pallas kernels for 0% -> 0%
where the time goes in v3:
time: 155 us; the launch traced here: 154 us
  Pallas kernels  129 us (83%)
  local copies, waits for them, and re-layouts  6.74 us (4%)
  starting transfers between devices  6.34 us (4%)
  other arithmetic  4.79 us (3%)
  matrix products  4.44 us (3%)
  waiting for transfers between devices  2.94 us (2%)
    pallas_call x1, Pallas kernels, expert_rows(): pl.pallas_call(expert_kernel, out_shape=jax.ShapeDtypeStruct((owned, rows...  67.9 us
    pallas_call x1, Pallas kernels, combine_plane(): pl.pallas_call(combine_kernel, out_shape=jax.ShapeDtypeStruct((tok // n,...  32.9 us
    pallas_call x1, Pallas kernels, gather_plane(): pl.pallas_call(gather_kernel, out_shape=jax.ShapeDtypeStruct((4, tok, col...  28.1 us
    ppermute x2, starting transfers between devices, shift(): lax.ppermute(x, axis, [(i, i + distance) for i in range(n - distance)])  6.34 us
    dot_general x1, matrix products, per_device(): jnp.dot(pick.reshape(owned * rows, n_seq * tok), tokens, preferred_elemen...  3.76 us
  transfers between devices with their start and end apart: 4, of which 2 were waited for; matrix products, arithmetic and copies ran while one was open for 5% of the time, Pallas kernels for 0%

profile of v3, /device:TPU:0, one launch (start us, length us, event | category | flops | bytes accessed | tf_op | source)
XLA Modules:
  0.0 154.3 jit_solution(12509766213732747600)
XLA Ops:
  0.0 0.9 constant_dynamic-slice_fusion.1
  0.9 4.9 %collective-permute-start.2 = (bf16[128,256]{1,0:T(8,128)(2,1)S(1)}, bf16[128,256]{1,0:T(8,128)(2,1)S(1)}, u32[]{:S(2)}, u32[]{:S(2)}) collective-permute-start(bf16[128,256]{1,0:T(8,128)(2,1)S(1)} %pad_maximum_fusion), channel_id=1, source_target_pairs={{0,16},{8,24},{1,17},{9,25},{2,18},{10,26},{3,19},{11,27},{4,20},{... | collective-permute-start | bytes 196616 | tf_op jit(solution)/shard_map/ppermute | solution.py:28
  5.8 1.5 collective-permute-start.3
  7.3 0.7 convert_bitcast_fusion
  8.0 0.7 fusion.12
  8.6 0.0 collective-permute-start
  8.7 0.8 reduce-window.8
  9.5 0.1 convert_reduce_fusion
  9.6 0.1 convert_reduce_fusion.1
  9.7 0.1 broadcast_bitcast_fusion
  9.8 0.0 copy-done
  9.8 0.2 and_and_fusion
  10.1 2.2 %collective-permute-done = f32[1,8,128]{2,1,0:T(8,128)S(1)} collective-permute-done((f32[1,8,128]{2,1,0:T(8,128)S(1)}, f32[1,8,128]{2,1,0:T(8,128)S(1)}, u32[]{:S(2)}, u32[]{:S(2)}) %collective-permute-start) | collective-permute-done | bytes 4128 | tf_op jit(solution)/shard_map/ppermute | solution.py:23
  12.3 0.0 collective-permute-start.1
  12.3 0.2 copy.54
  12.4 0.1 broadcast_in_dim.93
  12.5 0.1 broadcast_in_dim.94
  12.6 0.1 eq.85
  12.7 0.8 collective-permute-done.1
  13.4 0.1 compare_reduce_fusion
  13.6 0.1 reduce_or.14
  13.6 1.2 reduce_window_sum.22
  14.9 0.1 reduce_window_sum.23
  14.9 0.1 fusion.6
  15.0 0.6 gather_fusion
  15.6 0.1 gather.13
  15.7 0.1 eq.82
  15.9 0.4 copy.41
  16.3 0.1 fusion.4
  16.4 0.1 reshape.311
  16.5 0.6 gather_fusion.1
  17.1 0.1 gather.15
  17.2 0.3 copy.44
  17.5 0.2 select_convert_fusion.spread
  17.7 0.2 broadcast_compare_fusion
  18.0 0.0 collective-permute-done.2
  18.0 0.0 collective-permute-done.3
  18.0 0.3 fusion.16
  18.3 0.2 fusion.2
  18.5 0.4 convolution_convert_fusion.1
  18.9 0.1 copy.49.own
  19.0 28.1 %shard_map.82 = bf16[4,128,3072]{2,1,0:T(8,128)(2,1)S(1)} custom-call(bf16[128,768]{1,0:T(8,128)(2,1)S(1)} %copy.49.own), custom_call_target="tpu_custom_call" | custom-call | tf_op jit(solution)/shard_map/pallas_call | solution.py:329
  47.1 3.8 %convolution_convert_fusion = bf16[576,3072]{1,0:T(8,128)(2,1)} fusion(pred[576,512]{1,0:T(8,128)(4,1)S(1)} %bitcast.82, bf16[512,3072]{1,0:T(8,128)(2,1)S(1)} %bitcast.75), kind=kOutput, calls=%fused_computation.2 | convolution fusion | flops 1813708800 | bytes 6979584 | tf_op jit(solution)/shard_map/dot_general | solution.py:476
  50.9 67.9 %shard_map.83 = bf16[4,144,3072]{2,1,0:T(8,128)(2,1)} custom-call(bf16[4,144,3072]{2,1,0:T(8,128)(2,1)} %bitcast.79, bf16[8,1344,3072]{2,1,0:T(8,128)(2,1)} %bitcast.76, bf16[4,1344,3072]{2,1,0:T(8,128)(2,1)} %bitcast.77), custom_call_target="tpu_custom_call" | custom-call | flops 14269022208 | bytes 99090432 | tf_op jit(solution)/shard_map/pallas_call | solution.py:228
  118.8 0.0 copy-start.2
  118.8 2.0 %copy-done.2 = bf16[4,144,3072]{2,1,0:T(8,128)(2,1)S(1)} copy-done((bf16[4,144,3072]{2,1,0:T(8,128)(2,1)S(1)}, bf16[4,144,3072]{2,1,0:T(8,128)(2,1)}, u32[]{:S(2)}) %copy-start.2) | copy-done | bytes 3538968
  120.8 32.9 %shard_map.84 = bf16[32,3072]{1,0:T(8,128)(2,1)S(1)} custom-call(bf16[512,576]{1,0:T(8,128)(2,1)S(1)} %select_convert_fusion.spread, bf16[576,3072]{1,0:T(8,128)(2,1)S(1)} %bitcast.74), custom_call_target="tpu_custom_call" | custom-call | tf_op jit(solution)/shard_map/pallas_call | solution.py:411
  153.6 0.7 copy.66
  (27 shorter events, 0.2 us)
Async XLA Ops:
  0.0 9.8 %copy-start = (bf16[128,6144]{1,0:T(8,128)(2,1)S(1)}, bf16[128,6144]{1,0:T(8,128)(2,1)}, u32[]{:S(2)}) copy-start(bf16[128,6144]{1,0:T(8,128)(2,1)} %param.8) | copy-start | bytes 4718596
  0.9 17.0 %collective-permute-start.2 = (bf16[128,256]{1,0:T(8,128)(2,1)S(1)}, bf16[128,256]{1,0:T(8,128)(2,1)S(1)}, u32[]{:S(2)}, u32[]{:S(2)}) collective-permute-start(bf16[128,256]{1,0:T(8,128)(2,1)S(1)} %pad_maximum_fusion), channel_id=1, source_target_pairs={{0,16},{8,24},{1,17},{9,25},{2,18},{10,26},{3,19},{11,27},{4,20},{... | collective-permute-start | bytes 196616 | tf_op jit(solution)/shard_map/ppermute | solution.py:28
  5.8 12.2 %collective-permute-start.3 = (bf16[128,256]{1,0:T(8,128)(2,1)S(1)}, bf16[128,256]{1,0:T(8,128)(2,1)S(1)}, u32[]{:S(2)}, u32[]{:S(2)}) collective-permute-start(bf16[128,256]{1,0:T(8,128)(2,1)S(1)} %pad_maximum_fusion), channel_id=1, source_target_pairs={{0,8},{8,16},{16,24},{1,9},{9,17},{17,25},{2,10},{10,18},{18,26},{... | collective-permute-start | bytes 196616 | tf_op jit(solution)/shard_map/ppermute | solution.py:28
  8.6 3.6 %collective-permute-start = (f32[1,8,128]{2,1,0:T(8,128)S(1)}, f32[1,8,128]{2,1,0:T(8,128)S(1)}, u32[]{:S(2)}, u32[]{:S(2)}) collective-permute-start(f32[1,8,128]{2,1,0:T(8,128)S(1)} %get-tuple-element.10), channel_id=1, source_target_pairs={{0,16},{8,24},{16,0},{24,8},{1,17},{9,25},{17,1},{25,9},{2,18},{10... | collective-permute-start | bytes 12296 | tf_op jit(solution)/shard_map/ppermute | solution.py:23
  12.3 1.2 collective-permute-start.1
  118.8 2.0 %copy-start.2 = (bf16[4,144,3072]{2,1,0:T(8,128)(2,1)S(1)}, bf16[4,144,3072]{2,1,0:T(8,128)(2,1)}, u32[]{:S(2)}) copy-start(bf16[4,144,3072]{2,1,0:T(8,128)(2,1)} %shard_map.83) | copy-start | bytes 10616836
  120.8 33.6 %copy-start.1 = (bf16[128,6144]{1,0:T(8,128)(2,1)S(1)}, bf16[128,6144]{1,0:T(8,128)(2,1)}, u32[]{:S(2)}) copy-start(bf16[128,6144]{1,0:T(8,128)(2,1)} %param.8) | copy-start | bytes 4718596

commit v4 on v3

--- a/solution.py
+++ b/solution.py
@@ -103,7 +103,7 @@
     return full.reshape(n_seq * tok, cols)
 
 
-def expert_kernel(p_ref, wg_ref, wd_ref, out_ref, wbuf, kept, sent, got, hid, wsem, s1, r1, s2, r2):
+def expert_kernel(pick_ref, tok_ref, wg_ref, wd_ref, out_ref, p_ref, wbuf, kept, sent, got, hid, wsem, s1, r1, s2, r2):
     r = lax.axis_index("rep")
     partner = {"rep": 1 - r}
     owned, rows, cols = out_ref.shape
@@ -127,6 +127,13 @@
         if t + SLOTS < len(blocks):
             load(t + SLOTS).start()
 
+    def pick_rows(e):
+        @pl.loop(0, cols // D_STEP)
+        def _(k):
+            at = pl.ds(pl.multiple_of(k * D_STEP, D_STEP), D_STEP)
+            acc = jnp.dot(pick_ref[e], tok_ref[:, at], preferred_element_type=jnp.float32)
+            p_ref[e, :, at] = acc.astype(jnp.bfloat16)
+
     def gate_part(t, e, dst):
         load(t).wait()
         w = wbuf.at[t % SLOTS]
@@ -184,11 +191,13 @@
 
     t = 0
     for p in range(pairs):
+        pick_rows(theirs[p])
         for g in range(2):
             gate_part(t, theirs[p], sent.at[p, g])
             reduce_copy(p, g).start()
             t += 1
     for p in range(pairs):
+        pick_rows(mine[p])
         for g in range(2):
             gate_part(t, mine[p], kept.at[p, g])
             t += 1
@@ -216,8 +225,9 @@
         hidden_copy(p).wait_send()
 
 
-def expert_rows(picked, gate_up, down_t):
-    owned, rows, cols = picked.shape
+def expert_rows(pick, tokens, gate_up, down_t):
+    owned, rows, _ = pick.shape
+    cols = tokens.shape[1]
     hidden = gate_up.shape[3]
     pairs = owned // 2
     wg = gate_up.transpose(0, 2, 3, 1).reshape(owned * 2, hidden, cols)
@@ -228,9 +238,10 @@
     return pl.pallas_call(
         expert_kernel,
         out_shape=jax.ShapeDtypeStruct((owned, rows, cols), jnp.bfloat16),
-        in_specs=[vmem, hbm, hbm],
+        in_specs=[vmem, vmem, hbm, hbm],
         out_specs=vmem,
         scratch_shapes=[
+            pltpu.VMEM((owned, rows, cols), jnp.bfloat16),
             pltpu.VMEM((SLOTS, hidden, cols), jnp.bfloat16),
             pltpu.VMEM(half, jnp.bfloat16),
             pltpu.VMEM(half, jnp.bfloat16),
@@ -250,7 +261,7 @@
             bytes_accessed=6 * owned * cols * hidden,
             transcendentals=owned * rows * hidden,
         ),
-    )(picked, wg, wd)
+    )(pick, tokens, wg, wd)
 
 
 def greet(partners):
@@ -473,10 +484,7 @@
         tokens = gather_tokens(own, tok, cols, split)
 
     if paired:
-        picked = jnp.dot(
-            pick.reshape(owned * rows, n_seq * tok), tokens, preferred_element_type=jnp.float32
-        ).astype(jnp.bfloat16)
-        outs = expert_rows(picked.reshape(owned, rows, cols), gate_up, down_t)
+        outs = expert_rows(pick, tokens, gate_up, down_t)
         outs = outs.reshape(owned * rows, cols)
     else:
         outs = []

time: 155 us -> 153 us (0.987)
  matrix products: 4.44 us -> 0.68 us
  local copies, waits for them, and re-layouts: 6.74 us -> 8.4 us
    dot_general x1 -> x0, matrix products: 3.76 us -> none  [per_device(): jnp.dot(pick.reshape(owned * rows, n_seq * tok), tokens, preferred_elemen...]
    unnamed x8 -> x10, local copies, waits for them, and re-layouts: 2.84 us -> 4.5 us
where the time goes in v4:
time: 153 us
  Pallas kernels  129 us (84%)
  local copies, waits for them, and re-layouts  8.4 us (5%)
  starting transfers between devices  6.34 us (4%)
  other arithmetic  5.55 us (4%)
  waiting for transfers between devices  2.94 us (2%)
    pallas_call x1, Pallas kernels, expert_rows(): pl.pallas_call(expert_kernel, out_shape=jax.ShapeDtypeStruct((owned, rows...  67.9 us
    pallas_call x1, Pallas kernels, combine_plane(): pl.pallas_call(combine_kernel, out_shape=jax.ShapeDtypeStruct((tok // n,...  32.9 us
    pallas_call x1, Pallas kernels, gather_plane(): pl.pallas_call(gather_kernel, out_shape=jax.ShapeDtypeStruct((4, tok, col...  28.1 us
    ppermute x2, starting transfers between devices, shift(): lax.ppermute(x, axis, [(i, i + distance) for i in range(n - distance)])  6.34 us
    unnamed x10, local copies, waits for them, and re-layouts  4.5 us
  transfers between devices with their start and end apart: 4, of which 2 were waited for; matrix products, arithmetic and copies ran while one was open for 5% of the time, Pallas kernels for 0%

profile of v4, /device:TPU:0, one launch (start us, length us, event | category | flops | bytes accessed | tf_op | source)
XLA Modules:
  0.0 153.0 jit_solution(9717998557942668194)
XLA Ops:
  0.0 0.0 copy-start
  0.0 0.9 constant_dynamic-slice_fusion.1
  0.9 4.9 %collective-permute-start.2 = (bf16[128,256]{1,0:T(8,128)(2,1)S(1)}, bf16[128,256]{1,0:T(8,128)(2,1)S(1)}, u32[]{:S(2)}, u32[]{:S(2)}) collective-permute-start(bf16[128,256]{1,0:T(8,128)(2,1)S(1)} %pad_maximum_fusion), channel_id=1, source_target_pairs={{0,16},{8,24},{1,17},{9,25},{2,18},{10,26},{3,19},{11,27},{4,20},{... | collective-permute-start | bytes 196616 | tf_op jit(solution)/shard_map/ppermute | solution.py:28
  5.8 1.5 collective-permute-start.3
  7.3 0.7 convert_bitcast_fusion
  8.0 0.7 fusion.12
  8.6 0.0 collective-permute-start
  8.7 0.8 reduce-window.8
  9.5 0.1 convert_reduce_fusion
  9.6 0.1 convert_reduce_fusion.1
  9.7 0.1 broadcast_bitcast_fusion
  9.8 0.2 and_and_fusion
  10.1 2.2 %collective-permute-done = f32[1,8,128]{2,1,0:T(8,128)S(1)} collective-permute-done((f32[1,8,128]{2,1,0:T(8,128)S(1)}, f32[1,8,128]{2,1,0:T(8,128)S(1)}, u32[]{:S(2)}, u32[]{:S(2)}) %collective-permute-start) | collective-permute-done | bytes 4128 | tf_op jit(solution)/shard_map/ppermute | solution.py:23
  12.3 0.0 collective-permute-start.1
  12.3 0.2 copy.54
  12.4 0.1 broadcast_in_dim.93
  12.5 0.1 broadcast_in_dim.94
  12.6 0.1 eq.75
  12.7 0.8 collective-permute-done.1
  13.4 0.1 compare_reduce_fusion
  13.6 0.1 reduce_or.14
  13.6 1.2 reduce_window_sum.22
  14.9 0.1 reduce_window_sum.23
  14.9 0.1 fusion.6
  15.0 0.6 gather_fusion
  15.6 0.1 gather.13
  15.7 0.1 eq.72
  15.9 0.4 copy.41
  16.3 0.1 fusion.4
  16.4 0.1 reshape.275
  16.5 0.6 gather_fusion.1
  17.1 0.1 gather.15
  17.2 0.3 copy.44
  17.5 0.2 select_convert_fusion.spread
  17.7 1.0 compare_convert_fusion.pick_ref
  18.7 0.0 collective-permute-done.2
  18.7 0.0 collective-permute-done.3
  18.7 0.3 fusion.16
  19.1 0.2 fusion.2
  19.2 0.4 convolution_convert_fusion
  19.6 0.1 copy.49.own
  19.8 28.1 %shard_map.82 = bf16[4,128,3072]{2,1,0:T(8,128)(2,1)S(1)} custom-call(bf16[128,768]{1,0:T(8,128)(2,1)S(1)} %copy.49.own), custom_call_target="tpu_custom_call" | custom-call | tf_op jit(solution)/shard_map/pallas_call | solution.py:340
  47.9 0.0 copy-start.3
  47.9 1.7 %copy-done.3 = bf16[4,128,3072]{2,1,0:T(8,128)(2,1)} copy-done((bf16[4,128,3072]{2,1,0:T(8,128)(2,1)}, bf16[4,128,3072]{2,1,0:T(8,128)(2,1)S(1)}, u32[]{:S(2)}) %copy-start.3) | copy-done | bytes 3145752
  49.5 67.9 %shard_map.83 = bf16[4,144,3072]{2,1,0:T(8,128)(2,1)} custom-call(bf16[4,144,512]{2,1,0:T(8,128)(2,1)} %compare_convert_fusion.pick_ref, bf16[512,3072]{1,0:T(8,128)(2,1)} %bitcast.71, bf16[8,1344,3072]{2,1,0:T(8,128)(2,1)} %bitcast.72, bf16[4,1344,3072]{2,1,0:T(8,128)(2,1)} %bitcast.73), custom_call_target="tpu_custom_call" | custom-call | flops 14269022208 | bytes 99090432 | tf_op jit(solution)/shard_map/pallas_call | solution.py:238
  117.4 2.0 %copy-done.2 = bf16[4,144,3072]{2,1,0:T(8,128)(2,1)S(1)} copy-done((bf16[4,144,3072]{2,1,0:T(8,128)(2,1)S(1)}, bf16[4,144,3072]{2,1,0:T(8,128)(2,1)}, u32[]{:S(2)}) %copy-start.2) | copy-done | bytes 3538968
  119.4 32.9 %shard_map.84 = bf16[32,3072]{1,0:T(8,128)(2,1)S(1)} custom-call(bf16[512,576]{1,0:T(8,128)(2,1)S(1)} %select_convert_fusion.spread, bf16[576,3072]{1,0:T(8,128)(2,1)S(1)} %bitcast.70), custom_call_target="tpu_custom_call" | custom-call | tf_op jit(solution)/shard_map/pallas_call | solution.py:422
  152.3 0.7 copy.66
  (28 shorter events, 0.2 us)
Async XLA Ops:
  0.0 9.8 %copy-start = (bf16[128,6144]{1,0:T(8,128)(2,1)S(1)}, bf16[128,6144]{1,0:T(8,128)(2,1)}, u32[]{:S(2)}) copy-start(bf16[128,6144]{1,0:T(8,128)(2,1)} %param.8) | copy-start | bytes 4718596
  0.9 17.8 %collective-permute-start.2 = (bf16[128,256]{1,0:T(8,128)(2,1)S(1)}, bf16[128,256]{1,0:T(8,128)(2,1)S(1)}, u32[]{:S(2)}, u32[]{:S(2)}) collective-permute-start(bf16[128,256]{1,0:T(8,128)(2,1)S(1)} %pad_maximum_fusion), channel_id=1, source_target_pairs={{0,16},{8,24},{1,17},{9,25},{2,18},{10,26},{3,19},{11,27},{4,20},{... | collective-permute-start | bytes 196616 | tf_op jit(solution)/shard_map/ppermute | solution.py:28
  5.8 12.9 %collective-permute-start.3 = (bf16[128,256]{1,0:T(8,128)(2,1)S(1)}, bf16[128,256]{1,0:T(8,128)(2,1)S(1)}, u32[]{:S(2)}, u32[]{:S(2)}) collective-permute-start(bf16[128,256]{1,0:T(8,128)(2,1)S(1)} %pad_maximum_fusion), channel_id=1, source_target_pairs={{0,8},{8,16},{16,24},{1,9},{9,17},{17,25},{2,10},{10,18},{18,26},{... | collective-permute-start | bytes 196616 | tf_op jit(solution)/shard_map/ppermute | solution.py:28
  8.6 3.6 %collective-permute-start = (f32[1,8,128]{2,1,0:T(8,128)S(1)}, f32[1,8,128]{2,1,0:T(8,128)S(1)}, u32[]{:S(2)}, u32[]{:S(2)}) collective-permute-start(f32[1,8,128]{2,1,0:T(8,128)S(1)} %get-tuple-element.10), channel_id=1, source_target_pairs={{0,16},{8,24},{16,0},{24,8},{1,17},{9,25},{17,1},{25,9},{2,18},{10... | collective-permute-start | bytes 12296 | tf_op jit(solution)/shard_map/ppermute | solution.py:23
  12.3 1.2 collective-permute-start.1
  47.9 1.7 %copy-start.3 = (bf16[4,128,3072]{2,1,0:T(8,128)(2,1)}, bf16[4,128,3072]{2,1,0:T(8,128)(2,1)S(1)}, u32[]{:S(2)}) copy-start(bf16[4,128,3072]{2,1,0:T(8,128)(2,1)S(1)} %shard_map.82) | copy-start | bytes 9437188
  117.4 2.0 %copy-start.2 = (bf16[4,144,3072]{2,1,0:T(8,128)(2,1)S(1)}, bf16[4,144,3072]{2,1,0:T(8,128)(2,1)}, u32[]{:S(2)}) copy-start(bf16[4,144,3072]{2,1,0:T(8,128)(2,1)} %shard_map.83) | copy-start | bytes 10616836
  119.4 33.6 %copy-start.1 = (bf16[128,6144]{1,0:T(8,128)(2,1)S(1)}, bf16[128,6144]{1,0:T(8,128)(2,1)}, u32[]{:S(2)}) copy-start(bf16[128,6144]{1,0:T(8,128)(2,1)} %param.8) | copy-start | bytes 4718596
